TPU v7x, 128 devices: a whole 4x4x4 slice. The times are simulated.
128 devices in a mesh: gx: 8 (over x, core), gy: 16 (over y, z).
Axes of the slice: x: 4, y: 4, z: 4, core: 2. Of those that a mesh axis runs over, the one named last changes fastest.
Arguments:
- right_side: float32 [216, 65536], P(None, ('gx', 'gy')), may hold values from -15 to 15
- stiffness: float32 [3, 216, 216], replicated, may hold values from -6.5 to 8, as said below
- metric: float32 [3, 65536], P(None, ('gx', 'gy')), may hold values from 0.2 to 2
- levels: int32 [65536], P(('gx', 'gy')), may hold values from 0 to 2
- projection: float32 [4, 36, 36], replicated, may hold values from -1 to 1
- mortar_fine: int32 [65536], P(('gx', 'gy')), may hold values from 0 to 511, as said below
- mortar_face: int32 [65536], P(('gx', 'gy')), may hold values from 0 to 5
- mortar_owner: int32 [65536, 1], P(('gx', 'gy')), may hold values from 0 to 127, as said below
- mortar_subface: int32 [65536], P(('gx', 'gy')), may hold values from 0 to 3
- mortar_coarse: int32 [65536], P(('gx', 'gy')), may hold values from 0 to 511, as said below
- mortar_cface: int32 [65536], P(('gx', 'gy')), may hold values from 0 to 5
Outputs:
- solution_field: float32 [216, 65536], P(None, ('gx', 'gy'))
- residual: float32 [216, 65536], P(None, ('gx', 'gy'))
Inputs may be any that keep to these rules, and one draw needn't show every extreme that they name: `stiffness`: symmetric; positive definite. `mortar_owner`: A device index in mesh order: the device that holds the fine element or one of its neighbours in the grid of devices, diagonal ones included. Exactly 128 of one device's 512 faces name that device itself, at most 128 name any one neighbour, and each neighbour of a corner device is named exactly 128 times by it. `mortar_fine`: where the owner is another device, an element on the edge of the block that faces the owner: a = 0 or 3 toward a neighbour along the first direction, b = 0 or 127 along the second. `mortar_coarse`: where the owner is another device, the owner's element across that edge or corner from the fine element; where the owner is the device itself, any element.
All inputs are finite; a program needn't handle non-finite values.
Results may differ from a plain program's by a relative error of at most 0.0003.
Values sent between devices are 32-bit elements; how exact they have to be, the bound alone decides.
A program may use at most 64 MiB of HBM per device.

v0:
```python
import functools

import jax
import jax.numpy as jnp
import numpy as np
from jax import lax
from jax.experimental import pallas as pl
from jax.experimental.pallas import tpu as pltpu
from jax.sharding import PartitionSpec as P

NP = 6
NODES = NP * NP * NP
SIDE = NP * NP
EA = 4
EB = 128
ELEMS = EA * EB
FR = 40
FACES = 6 * FR
PENALTY = 1.0

F32 = jnp.float32
BF16 = jnp.bfloat16
MESH = pl.DeviceIdType.MESH

DIRS = {d: (d // 3 - 1, d % 3 - 1) for d in range(9) if d != 4}
EDGE_DIRS = (3, 5, 0, 2, 6, 8)
EDGE_BASE = {3: 0, 5: 4, 0: 8, 2: 9, 6: 10, 8: 11}


def face_nodes(face):
    ids = np.arange(NODES).reshape(NP, NP, NP)
    return [ids[0], ids[5], ids[:, 0], ids[:, 5], ids[:, :, 0], ids[:, :, 5]][face].reshape(-1)


def constant_tables():
    pick = np.zeros((FACES, NODES), np.float32)
    for face in range(6):
        pick[face * FR + np.arange(SIDE), face_nodes(face)] = 1.0
    edge = np.zeros((ELEMS, 128), np.float32)
    columns = [a * EB for a in range(EA)] + [a * EB + EB - 1 for a in range(EA)]
    columns += [0, EB - 1, (EA - 1) * EB, ELEMS - 1]
    for face in range(6):
        for pair, column in enumerate(columns):
            edge[column, face * 16 + pair] = 1.0
    return pick, pick.T.copy(), edge


def dot(a, b):
    return lax.dot_general(a, b, (((1,), (0,)), ((), ())), preferred_element_type=F32)


def dot_nt(a, b):
    return lax.dot_general(a, b, (((1,), (1,)), ((), ())), preferred_element_type=F32)


def split(value):
    high = value.astype(BF16)
    return high, (value - high.astype(F32)).astype(BF16)


def iota(shape, dim):
    return lax.broadcasted_iota(jnp.int32, shape, dim)


def one_hot(rows, code):
    return jnp.where(iota((rows, code.shape[1]), 0).astype(F32) == code, 1.0, 0.0).astype(BF16)


def pick_face(sides, face):
    out = None
    for f in range(6):
        part = jnp.where(face == float(f), sides[f * FR : (f + 1) * FR], 0.0)
        out = part if out is None else out + part
    return out


def spread_face(values, face):
    return jnp.concatenate([jnp.where(face == float(f), values, 0.0) for f in range(6)], axis=0)


def spread_split(values, face):
    high = values.astype(BF16).astype(F32)
    return spread_face(high, face).astype(BF16), spread_face(values - high, face).astype(BF16)


def by_subface(values, sub):
    return jnp.concatenate([jnp.where(sub == float(s), values, 0.0) for s in range(4)], axis=0).astype(BF16)


def column_sums(a, b):
    prod = a * b
    rows = jnp.sum(prod, axis=0, keepdims=True)
    return sum(rows[:, t * EB : (t + 1) * EB] for t in range(EA))


def kernel(
    n_gx,
    n_gy,
    b_ref,
    stiff_ref,
    metric_ref,
    ints_ref,
    proj_ref,
    pick_ref,
    place_ref,
    edge_ref,
    x_ref,
    r_ref,
    fld,
    halo_x,
    halo_y,
    halo_m,
    own_m,
    own_y,
    stiff_h,
    stiff_l,
    oh_self,
    oh_x,
    n_out,
    n_in,
    proj_s,
    proj_c,
    proj_t,
    red1,
    red2,
    mine1,
    mine2,
    sx_send,
    sx_recv,
    sy_send,
    sy_recv,
    sm_send,
    sm_recv,
    s1_send,
    s1_recv,
    s2_send,
    s2_recv,
):
    gx = lax.axis_index("gx")
    gy = lax.axis_index("gy")

    def there(d):
        dx, dy = DIRS[d]
        ok = (gx + dx >= 0) & (gx + dx < n_gx) & (gy + dy >= 0) & (gy + dy < n_gy)
        return ok, {"gx": gx + dx, "gy": gy + dy}

    halo_x[...] = jnp.zeros_like(halo_x)
    halo_y[...] = jnp.zeros_like(halo_y)
    halo_m[...] = jnp.zeros_like(halo_m)

    barrier = pltpu.get_barrier_semaphore()
    for k in range(1, n_gx):
        pl.semaphore_signal(barrier, inc=1, device_id={"gx": lax.rem(gx + k, n_gx), "gy": gy}, device_id_type=MESH)
    for k in range(1, n_gy):
        pl.semaphore_signal(barrier, inc=1, device_id={"gx": gx, "gy": lax.rem(gy + k, n_gy)}, device_id_type=MESH)
    expected = jnp.int32(n_gx + n_gy - 2)
    for d in (0, 2, 6, 8):
        ok, where = there(d)

        @pl.when(ok)
        def _():
            pl.semaphore_signal(barrier, inc=1, device_id=where, device_id_type=MESH)

        expected = expected + ok.astype(jnp.int32)
    pl.semaphore_wait(barrier, expected)

    def x_copy(t, side, arriving):
        d = (1, 7)[side]
        tile = (0, EA - 1)[side]
        slot = side if arriving else 1 - side
        return pltpu.make_async_remote_copy(
            src_ref=fld.at[t, :, pl.ds(tile * EB, EB)],
            dst_ref=halo_x.at[t, slot],
            send_sem=sx_send.at[t, side],
            recv_sem=sx_recv.at[t, slot],
            device_id=there(d)[1],
            device_id_type=MESH,
        )

    def y_copy(t, index, arriving):
        d = EDGE_DIRS[index]
        slot = index if arriving else EDGE_DIRS.index(8 - d)
        return pltpu.make_async_remote_copy(
            src_ref=own_y.at[t],
            dst_ref=halo_y.at[t, slot],
            send_sem=sy_send.at[t, index],
            recv_sem=sy_recv.at[t, slot],
            device_id=there(d)[1],
            device_id_type=MESH,
        )

    def m_copy(d, arriving):
        slot = d if arriving else 8 - d
        return pltpu.make_async_remote_copy(
            src_ref=own_m.at[d],
            dst_ref=halo_m.at[slot],
            send_sem=sm_send.at[d],
            recv_sem=sm_recv.at[slot],
            device_id=there(d)[1],
            device_id_type=MESH,
        )

    def if_there(d, act):
        pl.when(there(d)[0])(act)

    def send_x(t):
        for side in range(2):
            if_there((1, 7)[side], lambda: x_copy(t, side, False).start())

    fld[0] = b_ref[...]
    send_x(0)

    fine = ints_ref[0:1, :]
    face = ints_ref[1:2, :]
    owner = ints_ref[2:3, :]
    sub = ints_ref[3:4, :]
    coarse = ints_ref[4:5, :]
    cface = ints_ref[5:6, :]
    level = ints_ref[6:7, :]
    shift = n_gy.bit_length() - 1
    slot = ((owner >> shift) - gx + 1) * 3 + (owner & (n_gy - 1)) - gy + 1
    count = fine.shape[1]
    hits = jnp.where(iota((16, count), 0) == slot, 1.0, 0.0)
    before = jnp.where(iota((count, count), 0) < iota((count, count), 1), 1.0, 0.0).astype(BF16)
    position = jnp.sum(hits * dot(hits.astype(BF16), before), axis=0, keepdims=True)
    row = iota((8, count), 0)
    facts = jnp.ones((8, count), jnp.int32)
    for index, entry in enumerate((fine >> 7, fine & 127, face, coarse >> 7, coarse & 127, cface, sub)):
        facts = jnp.where(row == index, entry, facts)
    facts = facts.astype(F32)
    stacked = jnp.concatenate([facts * hits[k : k + 1] for k in range(9)], axis=0).astype(BF16)
    packed = dot_nt(stacked, one_hot(EB, position))
    for k in range(9):
        own_m[k] = packed[8 * k : 8 * k + 8]
    for d in DIRS:
        if_there(d, lambda: m_copy(d, False).start())

    for d in range(3):
        high, low = split(stiff_ref[d])
        stiff_h[d] = high
        stiff_l[d] = low
    proj_s[...] = jnp.zeros_like(proj_s)
    for s in range(4):
        proj_s[s * FR : s * FR + SIDE, 0:SIDE] = proj_ref[s]
    stack = proj_s[...]
    flipped = stack.T
    proj_t[...] = flipped[0:FR]
    proj_c[...] = jnp.zeros_like(proj_c)
    for s in range(4):
        proj_c[0:SIDE, s * FR : s * FR + SIDE] = proj_ref[s]
    scale = jnp.where(level == 0, 1.0, jnp.where(level == 1, 0.5, 0.25))

    def code(entry, active):
        return jnp.where(active > 0.0, entry, -1.0)

    me = own_m[4]
    self_fine = code(me[0:1] * float(EB) + me[1:2], me[7:8])
    self_coarse = code(me[3:4] * float(EB) + me[4:5], me[7:8])
    oh_self[...] = one_hot(ELEMS, jnp.concatenate([self_fine, self_coarse], axis=1))

    def edge_codes(held):
        parts_f, parts_c = [], []
        for d in EDGE_DIRS:
            facts_d = held[d]
            pair = facts_d[0:1] + float(EDGE_BASE[d]) if d in (3, 5) else float(EDGE_BASE[d])
            parts_f.append(code(facts_d[2:3] * 16.0 + pair, facts_d[7:8]))
            parts_c.append(code(facts_d[6:7] * 128.0 + facts_d[5:6] * 16.0 + pair, facts_d[7:8]))
        return (
            one_hot(128, jnp.concatenate(parts_f, axis=1)),
            one_hot(512, jnp.concatenate(parts_c, axis=1)),
        )

    ones = jnp.ones((16, 6 * EB), BF16)
    edge_f, edge_c = edge_codes(own_m)
    n_out[...] = dot_nt(edge_f, edge_c).astype(BF16)
    sum_out = dot_nt(ones, edge_f)[0:1]

    lane = iota((1, 128), 1)
    lane_face = lane >> 4
    lane_pair = lane & 15

    proj_s_h, proj_s_l = split(proj_s[0 : 4 * FR, 0:FR])
    proj_c_h, proj_c_l = split(proj_c[:, 0 : 4 * FR])
    proj_t_h, proj_t_l = split(proj_t[:, 0 : 4 * FR])

    def by_table(high, low, value_h, value_l):
        return dot(high, value_h) + dot(low, value_h) + dot(high, value_l)

    state = {}

    def first_lists():
        for d in DIRS:
            if_there(d, lambda: m_copy(d, True).wait_recv())
        for side in range(2):
            d = (1, 7)[side]
            both = jnp.concatenate([own_m[d], halo_m[d]], axis=1)
            oh_x[side] = one_hot(EB, code(both[1:2], both[7:8]))
        edge_f_in, edge_c_in = edge_codes(halo_m)
        n_in[...] = dot_nt(edge_f_in, edge_c_in).astype(BF16)
        state["sum_in"] = dot_nt(ones, edge_c_in)[0:1]

    def apply(t):
        pick = pick_ref[...]
        field = fld[t]
        field_h, field_l = split(field)
        f_h = dot(pick, field_h)
        f_l = dot(pick, field_l)
        faces = f_h + f_l
        f_h = f_h.astype(BF16)
        f_l = f_l.astype(BF16)
        edges = dot(f_h, edge_ref[...]) + dot(f_l, edge_ref[...])
        own = None
        for f in range(6):
            part = jnp.where(lane_face == f, edges[f * FR : (f + 1) * FR], 0.0)
            own = part if own is None else own + part
        own_y[t] = own
        for index in range(6):
            if_there(EDGE_DIRS[index], lambda: y_copy(t, index, False).start())

        total = field
        for d in range(3):
            total = total + metric_ref[d : d + 1, :] * by_table(stiff_h[d], stiff_l[d], field_h, field_l)
        total = scale * total

        got = dot(f_h, oh_self[...]) + dot(f_l, oh_self[...])
        fines = [pick_face(got[:, 0:EB], me[2:3])]
        coarses = [pick_face(got[:, EB:], me[5:6])]

        for side in range(2):
            if_there((1, 7)[side], lambda: x_copy(t, side, True).wait_recv())
        for index in range(6):
            if_there(EDGE_DIRS[index], lambda: y_copy(t, index, True).wait_recv())
        if t == 0:
            first_lists()

        halo_faces = []
        for side in range(2):
            tile = (0, EA - 1)[side]
            d = (1, 7)[side]
            h_h, h_l = split(halo_x[t, side])
            h_h = dot(pick, h_h)
            h_l = dot(pick, h_l)
            halo_faces.append(h_h + h_l)
            here = slice(tile * EB, (tile + 1) * EB)
            rows = jnp.concatenate([f_h[:, here], h_h.astype(BF16)], axis=0)
            rows_l = jnp.concatenate([f_l[:, here], h_l.astype(BF16)], axis=0)
            got = dot(rows, oh_x[side]) + dot(rows_l, oh_x[side])
            ours, theirs = got[0:FACES], got[FACES:]
            fines.append(pick_face(ours[:, 0:EB], own_m[d][2:3]))
            coarses.append(pick_face(theirs[:, 0:EB], own_m[d][5:6]))
            fines.append(pick_face(theirs[:, EB:], halo_m[d][2:3]))
            coarses.append(pick_face(ours[:, EB:], halo_m[d][5:6]))
        subs = jnp.concatenate(
            [me[6:7], own_m[1][6:7], halo_m[1][6:7], own_m[7][6:7], halo_m[7][6:7]], axis=1
        )
        fines = jnp.concatenate(fines, axis=1)
        coarses = jnp.concatenate(coarses, axis=1)
        c_high = coarses.astype(BF16).astype(F32)
        jump = by_table(proj_c_h, proj_c_l, by_subface(c_high, subs), by_subface(coarses - c_high, subs)) - fines

        def block(k):
            return jump[:, k * EB : (k + 1) * EB]

        returned = jnp.concatenate([block(0), block(2), block(4)], axis=1)
        back_subs = jnp.concatenate([me[6:7], halo_m[1][6:7], halo_m[7][6:7]], axis=1)
        j_high = returned.astype(BF16).astype(F32)
        back = by_table(proj_t_h, proj_t_l, by_subface(j_high, back_subs), by_subface(returned - j_high, back_subs))

        own_terms = jnp.concatenate([-PENALTY * block(0), PENALTY * back[:, 0:EB]], axis=1)
        s_h, s_l = spread_split(own_terms, jnp.concatenate([me[2:3], me[5:6]], axis=1))
        gathered = dot_nt(s_h, oh_self[...]) + dot_nt(s_l, oh_self[...])

        side_terms = []
        for side in range(2):
            d = (1, 7)[side]
            terms = jnp.concatenate(
                [-PENALTY * block(1 + 2 * side), PENALTY * back[:, (1 + side) * EB : (2 + side) * EB]], axis=1
            )
            s_h, s_l = spread_split(terms, jnp.concatenate([own_m[d][2:3], halo_m[d][5:6]], axis=1))
            side_terms.append(dot_nt(s_h, oh_x[side]) + dot_nt(s_l, oh_x[side]))

        across = jnp.zeros((FR, 128), F32)
        for index, (d, turn, low, high) in enumerate(
            ((3, -4, 0, 4), (5, 4, 4, 8), (0, -3, 8, 9), (2, -1, 9, 10), (6, 1, 10, 11), (8, 3, 11, 12))
        ):
            moved = pltpu.roll(halo_y[t, index], turn % 128, 1)
            across = jnp.where((lane_pair >= low) & (lane_pair < high), moved, across)
        pairs = jnp.concatenate([own, across], axis=1)
        pairs_h, pairs_l = split(pairs)
        images = by_table(proj_s_h, proj_s_l, pairs_h, pairs_l)
        image_own = jnp.concatenate([images[s * FR : (s + 1) * FR, 0:128] for s in range(4)], axis=1)
        image_far = jnp.concatenate([images[s * FR : (s + 1) * FR, 128:] for s in range(4)], axis=1)
        far_h, far_l = split(image_far)
        on_fine = own * sum_out - dot_nt(far_h, n_out[...]) - dot_nt(far_l, n_out[...])
        jumps = image_own * state["sum_in"] - dot(pairs_h[:, 128:], n_in[...]) - dot(pairs_l[:, 128:], n_in[...])
        jumps = jnp.concatenate([jumps[:, s * 128 : (s + 1) * 128] for s in range(4)], axis=0)
        jumps_h, jumps_l = split(jumps)
        on_edge = PENALTY * (on_fine + by_table(proj_t_h, proj_t_l, jumps_h, jumps_l))
        from_low = pltpu.roll(across, 128 - 16, 1)
        from_high = pltpu.roll(across, 16, 1)
        on_edge = on_edge - PENALTY * jnp.where(
            (lane_face == 2) & (lane_pair < 4),
            from_low,
            jnp.where((lane_face == 3) & (lane_pair >= 4) & (lane_pair < 8), from_high, 0.0),
        )
        e_high = on_edge.astype(BF16).astype(F32)
        e_low = on_edge - e_high
        e_h = jnp.concatenate([jnp.where(lane_face == f, e_high, 0.0) for f in range(6)], axis=0).astype(BF16)
        e_l = jnp.concatenate([jnp.where(lane_face == f, e_low, 0.0) for f in range(6)], axis=0).astype(BF16)
        gathered = gathered + dot_nt(e_h, edge_ref[...]) + dot_nt(e_l, edge_ref[...])

        blocks = []
        for a in range(EA):
            here = slice(a * EB, (a + 1) * EB)
            x_low, x_high = faces[0:FR, here], faces[FR : 2 * FR, here]
            y_low, y_high = faces[2 * FR : 3 * FR, here], faces[3 * FR : 4 * FR, here]
            if a == 0:
                left = halo_faces[0][FR : 2 * FR]
            else:
                left = faces[FR : 2 * FR, (a - 1) * EB : a * EB]
            if a == EA - 1:
                right = halo_faces[1][0:FR]
            else:
                right = faces[0:FR, (a + 1) * EB : (a + 2) * EB]
            below = jnp.where(lane == 0, 0.0, pltpu.roll(y_high, 1, 1))
            above = jnp.where(lane == EB - 1, 0.0, pltpu.roll(y_low, EB - 1, 1))
            lateral = jnp.concatenate([x_low - left, x_high - right, y_low - below, y_high - above], axis=0)
            lateral = jnp.concatenate([PENALTY * lateral, jnp.zeros((2 * FR, EB), F32)], axis=0)
            lateral = lateral + gathered[:, here]
            if a == 0:
                lateral = lateral + side_terms[0]
            if a == EA - 1:
                lateral = lateral + side_terms[1]
            blocks.append(lateral)
        g_h, g_l = split(jnp.concatenate(blocks, axis=1))
        place = place_ref[...]
        return total + dot(place, g_h) + dot(place, g_l)

    b = b_ref[...]
    q = apply(0)
    fld[1] = q
    send_x(1)
    w = apply(1)
    q = fld[1]
    b = b_ref[...]

    row = iota((8, 128), 0)
    sums = jnp.zeros((8, 128), F32)
    for index, (left, right) in enumerate(((b, b), (b, q), (q, q), (b, w), (q, w))):
        sums = jnp.where(row == index, column_sums(left, right), sums)

    mine1[...] = sums

    def one_copy(k):
        return pltpu.make_async_remote_copy(
            src_ref=mine1,
            dst_ref=red1.at[k],
            send_sem=s1_send.at[k],
            recv_sem=s1_recv.at[k],
            device_id={"gx": lax.rem(gx + k, n_gx), "gy": gy},
            device_id_type=MESH,
        )

    def two_copy(k):
        return pltpu.make_async_remote_copy(
            src_ref=mine2,
            dst_ref=red2.at[k],
            send_sem=s2_send.at[k],
            recv_sem=s2_recv.at[k],
            device_id={"gx": gx, "gy": lax.rem(gy + k, n_gy)},
            device_id_type=MESH,
        )

    for k in range(1, n_gx):
        one_copy(k).start()
    total = mine1[...]
    for k in range(1, n_gx):
        one_copy(k).wait_recv()
        total = total + red1[k]
    mine2[...] = total
    for k in range(1, n_gy):
        two_copy(k).start()
    for k in range(1, n_gy):
        two_copy(k).wait_recv()
        total = total + red2[k]

    sums = jnp.sum(total, axis=1, keepdims=True)
    bb, bq, qq, bw, qw = (sums[i : i + 1] for i in range(5))
    alpha = bb / bq
    new = bb - 2.0 * alpha * bq + alpha * alpha * qq
    grow = 1.0 + new / bb
    alpha_next = new / (grow * grow * bq - grow * alpha * (bw + qq) + alpha * alpha * qw)
    first = alpha + alpha_next * grow
    second = alpha * alpha_next
    x_ref[...] = first * b - second * q
    r_ref[...] = b - first * q + second * w

    for t in range(2):
        for side in range(2):
            if_there((1, 7)[side], lambda: x_copy(t, side, False).wait_send())
        for index in range(6):
            if_there(EDGE_DIRS[index], lambda: y_copy(t, index, False).wait_send())
    for d in DIRS:
        if_there(d, lambda: m_copy(d, False).wait_send())
    for k in range(1, n_gx):
        one_copy(k).wait_send()
    for k in range(1, n_gy):
        two_copy(k).wait_send()


def body(
    n_gx,
    n_gy,
    right_side,
    stiffness,
    metric,
    levels,
    projection,
    mortar_fine,
    mortar_face,
    mortar_owner,
    mortar_subface,
    mortar_coarse,
    mortar_cface,
):
    ints = jnp.stack(
        [
            mortar_fine,
            mortar_face,
            mortar_owner[:, 0],
            mortar_subface,
            mortar_coarse,
            mortar_cface,
            levels,
            jnp.zeros_like(levels),
        ]
    )
    pick, place, edge = constant_tables()
    field = jax.ShapeDtypeStruct(right_side.shape, F32)
    vmem = pl.BlockSpec(memory_space=pltpu.VMEM)
    dma = pltpu.SemaphoreType.DMA
    return pl.pallas_call(
        functools.partial(kernel, n_gx, n_gy),
        out_shape=(field, field),
        in_specs=[vmem] * 8,
        out_specs=(vmem, vmem),
        scratch_shapes=[
            pltpu.VMEM((2, NODES, ELEMS), F32),
            pltpu.VMEM((2, 2, NODES, EB), F32),
            pltpu.VMEM((2, 6, FR, 128), F32),
            pltpu.VMEM((9, 8, 128), F32),
            pltpu.VMEM((9, 8, 128), F32),
            pltpu.VMEM((2, FR, 128), F32),
            pltpu.VMEM((3, NODES, NODES), BF16),
            pltpu.VMEM((3, NODES, NODES), BF16),
            pltpu.VMEM((ELEMS, 2 * EB), BF16),
            pltpu.VMEM((2, EB, 2 * EB), BF16),
            pltpu.VMEM((128, 512), BF16),
            pltpu.VMEM((128, 512), BF16),
            pltpu.VMEM((256, 128), F32),
            pltpu.VMEM((FR, 256), F32),
            pltpu.VMEM((FR, 256), F32),
            pltpu.VMEM((n_gx, 8, 128), F32),
            pltpu.VMEM((n_gy, 8, 128), F32),
            pltpu.VMEM((8, 128), F32),
            pltpu.VMEM((8, 128), F32),
            dma((2, 2)),
            dma((2, 2)),
            dma((2, 6)),
            dma((2, 6)),
            dma((9,)),
            dma((9,)),
            dma((n_gx,)),
            dma((n_gx,)),
            dma((n_gy,)),
            dma((n_gy,)),
        ],
        compiler_params=pltpu.CompilerParams(
            collective_id=0, has_side_effects=True, vmem_limit_bytes=48 * 1024 * 1024
        ),
    )(
        right_side,
        stiffness,
        metric,
        ints,
        projection,
        jnp.asarray(pick, BF16),
        jnp.asarray(place, BF16),
        jnp.asarray(edge, BF16),
    )


def solution(mesh):
    columns = P(None, ("gx", "gy"))
    faces = P(("gx", "gy"))
    in_specs = (columns, P(), columns, faces, P(), faces, faces, P(("gx", "gy"), None), faces, faces, faces)
    run = functools.partial(body, mesh.shape["gx"], mesh.shape["gy"])
    return jax.shard_map(run, mesh=mesh, in_specs=in_specs, out_specs=(columns, columns), check_vma=False)
```

profile of v0, /device:TPU:1, one launch (start us, length us, event | category | flops | bytes accessed | tf_op | source)
XLA Modules:
  0.0 41.1 jit_solution(16796034439565637445)
XLA Ops:
  0.6 0.0 copy-start.2
  0.7 0.9 %stack.27.ints_ref = s32[8,512]{1,0:T(8,128)S(1)} concatenate(s32[1,512]{1,0:T(1,128)} %bitcast.7, s32[1,512]{1,0:T(1,128)} %bitcast.8, s32[1,512]{1,0:T(1,128)} %bitcast.9, s32[1,512]{1,0:T(1,128)} %bitcast.10, s32[1,512]{1,0:T(1,128)} %bitcast.11, s32[1,512]{1,0:T(1,128)} %bitcast.12, s32[1,512]{1,0:T(1,128)} %bitcast.13, s32[1,512]{1,0:T(1,128)S(1)} %stack_broadcast_in_dim.3), dimensions={0} | concatenate | bytes 32768 | tf_op jit(solution)/shard_map/stack | solution.py:526
  1.5 0.0 copy-start.5
  1.5 0.9 %copy.16.proj_ref = f32[4,36,36]{2,1,0:T(8,128)S(1)} copy(f32[4,36,36]{2,0,1:T(4,128)} %param.18) | data formatting | bytes 41472 | tf_op args[4]
  2.4 0.0 copy-done.2
  2.4 0.0 copy-done.5
  2.4 0.0 copy-start
  2.4 1.1 %copy-done = f32[3,216,216]{2,1,0:T(8,128)S(1)} copy-done((f32[3,216,216]{2,1,0:T(8,128)S(1)}, f32[3,216,216]{2,1,0:T(8,128)}, u32[]{:S(2)}) %copy-start) | copy-done | bytes 559896
  3.5 0.0 copy-start.1
  3.5 1.0 %copy-done.1 = f32[216,512]{1,0:T(8,128)S(1)} copy-done((f32[216,512]{1,0:T(8,128)S(1)}, f32[216,512]{1,0:T(8,128)}, u32[]{:S(2)}) %copy-start.1) | copy-done | bytes 442392
  4.5 0.0 copy-start.3
  4.5 0.9 %copy-done.3 = bf16[240,216]{1,0:T(8,128)(2,1)S(1)} copy-done((bf16[240,216]{1,0:T(8,128)(2,1)S(1)}, bf16[240,216]{1,0:T(8,128)(2,1)}, u32[]{:S(2)}) %copy-start.3) | copy-done | bytes 103704
  5.4 0.0 copy-start.4
  5.4 0.9 %copy-done.4 = bf16[216,240]{1,0:T(8,128)(2,1)S(1)} copy-done((bf16[216,240]{1,0:T(8,128)(2,1)S(1)}, bf16[216,240]{1,0:T(8,128)(2,1)}, u32[]{:S(2)}) %copy-start.4) | copy-done | bytes 103704
  6.3 33.3 %shard_map.149 = (f32[216,512]{1,0:T(8,128)S(1)}, f32[216,512]{1,0:T(8,128)S(1)}) custom-call(f32[216,512]{1,0:T(8,128)S(1)} %copy-done.1, f32[3,216,216]{2,1,0:T(8,128)S(1)} %copy-done, f32[3,512]{1,0:T(4,128)S(1)} %copy-done.5, s32[8,512]{1,0:T(8,128)S(1)} %stack.27.ints_ref, f32[4,36,36]{2,1,0:T(8,128)S(1)} %copy.16.proj_ref, ...), custom_call_target="tpu_custom_call" | custom-call | tf_op jit(solution)/shard_map/pallas_call | solution.py:542
  39.6 0.8 %copy.19 = f32[216,512]{1,0:T(8,128)} copy(f32[216,512]{1,0:T(8,128)S(1)} %get-tuple-element.4) | data formatting | bytes 884736
  40.4 0.8 %copy.20 = f32[216,512]{1,0:T(8,128)} copy(f32[216,512]{1,0:T(8,128)S(1)} %get-tuple-element.5) | data formatting | bytes 884736
  (1 shorter events, 0.0 us)
Async XLA Ops:
  0.6 1.8 %copy-start.2 = (bf16[512,128]{1,0:T(8,128)(2,1)S(1)}, bf16[512,128]{1,0:T(8,128)(2,1)}, u32[]{:S(2)}) copy-start(bf16[512,128]{1,0:T(8,128)(2,1)} %constant.10.clone.edge_ref) | copy-start | bytes 393220
  1.5 0.9 %copy-start.5 = (f32[3,512]{1,0:T(4,128)S(1)}, f32[3,512]{1,0:T(4,128)}, u32[]{:S(2)}) copy-start(f32[3,512]{1,0:T(4,128)} %metric_ref.1) | copy-start | bytes 18436
  2.4 1.1 %copy-start = (f32[3,216,216]{2,1,0:T(8,128)S(1)}, f32[3,216,216]{2,1,0:T(8,128)}, u32[]{:S(2)}) copy-start(f32[3,216,216]{2,1,0:T(8,128)} %stiff_ref.1) | copy-start | bytes 1679620
  3.5 1.0 %copy-start.1 = (f32[216,512]{1,0:T(8,128)S(1)}, f32[216,512]{1,0:T(8,128)}, u32[]{:S(2)}) copy-start(f32[216,512]{1,0:T(8,128)} %b_ref.1) | copy-start | bytes 1327108
  4.5 0.9 %copy-start.3 = (bf16[240,216]{1,0:T(8,128)(2,1)S(1)}, bf16[240,216]{1,0:T(8,128)(2,1)}, u32[]{:S(2)}) copy-start(bf16[240,216]{1,0:T(8,128)(2,1)} %constant.8.clone.pick_ref) | copy-start | bytes 311044
  5.4 0.9 %copy-start.4 = (bf16[216,240]{1,0:T(8,128)(2,1)S(1)}, bf16[216,240]{1,0:T(8,128)(2,1)}, u32[]{:S(2)}) copy-start(bf16[216,240]{1,0:T(8,128)(2,1)} %constant.9.clone.place_ref) | copy-start | bytes 311044
where the time goes:
time: 41.4 us; the launch traced here: 41.1 us
  Pallas kernels  33.3 us (80%)
  local copies, waits for them, and re-layouts  7.19 us (17%)
  between operations  0.68 us (2%)
    pallas_call x1, Pallas kernels, body(): pl.pallas_call(functools.partial(kernel, n_gx, n_gy), out_shape=(field, f...  33.3 us
    unnamed x15, local copies, waits for them, and re-layouts  6.33 us
    another operation x2, local copies, waits for them, and re-layouts, body(): jnp.stack([mortar_fine, mortar_face, mortar_owner[:, 0], mortar_subface,...  0.86 us

commit v1 on v0

v1 whole, which is shorter than its diff:
```python
import functools

import jax
import jax.numpy as jnp
import numpy as np
from jax import lax
from jax.experimental import pallas as pl
from jax.experimental.pallas import tpu as pltpu
from jax.sharding import PartitionSpec as P

NP = 6
NODES = NP * NP * NP
SIDE = NP * NP
EA = 4
EB = 128
ELEMS = EA * EB
FR = 40
FACES = 6 * FR
PENALTY = 1.0

F32 = jnp.float32
BF16 = jnp.bfloat16
MESH = pl.DeviceIdType.MESH

DIRS = {d: (d // 3 - 1, d % 3 - 1) for d in range(9) if d != 4}
EDGE_DIRS = (3, 5, 0, 2, 6, 8)
EDGE_BASE = {3: 0, 5: 4, 0: 8, 2: 9, 6: 10, 8: 11}


def face_nodes(face):
    ids = np.arange(NODES).reshape(NP, NP, NP)
    return [ids[0], ids[5], ids[:, 0], ids[:, 5], ids[:, :, 0], ids[:, :, 5]][face].reshape(-1)


def constant_tables():
    pick = np.zeros((FACES, NODES), np.float32)
    for face in range(6):
        pick[face * FR + np.arange(SIDE), face_nodes(face)] = 1.0
    edge = np.zeros((ELEMS, 128), np.float32)
    columns = [a * EB for a in range(EA)] + [a * EB + EB - 1 for a in range(EA)]
    columns += [0, EB - 1, (EA - 1) * EB, ELEMS - 1]
    for face in range(6):
        for pair, column in enumerate(columns):
            edge[column, face * 16 + pair] = 1.0
    return pick, pick.T.copy(), edge


def dot(a, b):
    return lax.dot_general(a, b, (((1,), (0,)), ((), ())), preferred_element_type=F32)


def dot_nt(a, b):
    return lax.dot_general(a, b, (((1,), (1,)), ((), ())), preferred_element_type=F32)


def split(value):
    high = value.astype(BF16)
    return high, (value - high.astype(F32)).astype(BF16)


def iota(shape, dim):
    return lax.broadcasted_iota(jnp.int32, shape, dim)


def one_hot(rows, code):
    return jnp.where(iota((rows, code.shape[1]), 0).astype(F32) == code, 1.0, 0.0).astype(BF16)


def pick_face(sides, face):
    out = None
    for f in range(6):
        part = jnp.where(face == float(f), sides[f * FR : (f + 1) * FR], 0.0)
        out = part if out is None else out + part
    return out


def spread_face(values, face):
    return jnp.concatenate([jnp.where(face == float(f), values, 0.0) for f in range(6)], axis=0)


def spread_split(values, face):
    high = values.astype(BF16).astype(F32)
    return spread_face(high, face).astype(BF16), spread_face(values - high, face).astype(BF16)


def by_subface(values, sub):
    return jnp.concatenate([jnp.where(sub == float(s), values, 0.0) for s in range(4)], axis=0).astype(BF16)


def column_sums(a, b):
    prod = a * b
    rows = jnp.sum(prod, axis=0, keepdims=True)
    return sum(rows[:, t * EB : (t + 1) * EB] for t in range(EA))


def kernel(
    n_gx,
    n_gy,
    b_hbm,
    stiff_hbm,
    metric_hbm,
    fine_hbm,
    face_hbm,
    owner_hbm,
    sub_hbm,
    coarse_hbm,
    cface_hbm,
    level_hbm,
    proj_hbm,
    pick_hbm,
    place_hbm,
    edge_hbm,
    q_ref,
    w_ref,
    coef_ref,
    b_ref,
    stiff_ref,
    metric_ref,
    ints_ref,
    proj_ref,
    pick_ref,
    place_ref,
    edge_ref,
    halo_x,
    halo_y,
    halo_m,
    own_m,
    own_x,
    own_y,
    stiff_h,
    stiff_l,
    oh_self,
    oh_x,
    n_out,
    n_in,
    proj_s,
    proj_c,
    proj_t,
    red0,
    red1,
    mine0,
    mine1,
    in_sem,
    sx_send,
    sx_recv,
    sy_send,
    sy_recv,
    sm_send,
    sm_recv,
    s0_send,
    s0_recv,
    s1_send,
    s1_recv,
):
    gx = lax.axis_index("gx")
    gy = lax.axis_index("gy")

    def there(d):
        dx, dy = DIRS[d]
        ok = (gx + dx >= 0) & (gx + dx < n_gx) & (gy + dy >= 0) & (gy + dy < n_gy)
        return ok, {"gx": gx + dx, "gy": gy + dy}

    def if_there(d, act):
        pl.when(there(d)[0])(act)

    size_x, size_y, size_z = n_gx // 2, n_gy // 4, 4
    chips = [(i, j, k) for i in range(size_x) for j in range(size_y) for k in range(size_z)][1:]
    chips.sort(key=lambda c: -sum(min(v, n - v) for v, n in zip(c, (size_x, size_y, size_z))))

    def chip(offset):
        y, z = gy // size_z, lax.rem(gy, size_z)
        return {
            "gx": lax.rem(gx + 2 * offset[0], n_gx),
            "gy": lax.rem(y + offset[1], size_y) * size_z + lax.rem(z + offset[2], size_z),
        }

    halo_x[...] = jnp.zeros_like(halo_x)
    halo_y[...] = jnp.zeros_like(halo_y)
    halo_m[...] = jnp.zeros_like(halo_m)

    barrier = pltpu.get_barrier_semaphore()
    expected = jnp.int32(len(chips))
    for offset in chips:
        pl.semaphore_signal(barrier, inc=1, device_id=chip(offset), device_id_type=MESH)
    for d in (0, 2, 6, 8, 1, 7):
        ok, where = there(d)

        @pl.when(ok)
        def _():
            pl.semaphore_signal(barrier, inc=1, device_id=where, device_id_type=MESH)

        expected = expected + ok.astype(jnp.int32)

    int_names = (fine_hbm, face_hbm, owner_hbm, sub_hbm, coarse_hbm, cface_hbm, level_hbm)
    loads = [(source, ints_ref.at[k]) for k, source in enumerate(int_names)]
    loads += [(b_hbm, b_ref), (pick_hbm, pick_ref), (edge_hbm, edge_ref), (proj_hbm, proj_ref)]
    loads += [(stiff_hbm, stiff_ref), (metric_hbm, metric_ref), (place_hbm, place_ref)]
    loads = [pltpu.make_async_copy(source, target, in_sem.at[k]) for k, (source, target) in enumerate(loads)]
    for load in loads:
        load.start()

    def x_copy(t, side, arriving):
        slot = side if arriving else 1 - side
        return pltpu.make_async_remote_copy(
            src_ref=own_x.at[t, side],
            dst_ref=halo_x.at[t, slot],
            send_sem=sx_send.at[t, side],
            recv_sem=sx_recv.at[t, slot],
            device_id=there((1, 7)[side])[1],
            device_id_type=MESH,
        )

    def y_copy(t, index, arriving):
        d = EDGE_DIRS[index]
        slot = index if arriving else EDGE_DIRS.index(8 - d)
        return pltpu.make_async_remote_copy(
            src_ref=own_y.at[t],
            dst_ref=halo_y.at[t, slot],
            send_sem=sy_send.at[t, index],
            recv_sem=sy_recv.at[t, slot],
            device_id=there(d)[1],
            device_id_type=MESH,
        )

    def m_copy(d, arriving):
        slot = d if arriving else 8 - d
        return pltpu.make_async_remote_copy(
            src_ref=own_m.at[d],
            dst_ref=halo_m.at[slot],
            send_sem=sm_send.at[d],
            recv_sem=sm_recv.at[slot],
            device_id=there(d)[1],
            device_id_type=MESH,
        )

    lane = iota((1, 128), 1)
    lane_face = lane >> 4
    lane_pair = lane & 15

    def by_table(high, low, value_h, value_l):
        return dot(high, value_h) + dot(low, value_h) + dot(high, value_l)

    def code(entry, active):
        return jnp.where(active > 0.0, entry, -1.0)

    for load in loads[:7]:
        load.wait()
    fine, face, owner, sub, coarse, cface, level = (ints_ref[k] for k in range(7))
    shift = n_gy.bit_length() - 1
    slot = ((owner >> shift) - gx + 1) * 3 + (owner & (n_gy - 1)) - gy + 1
    count = fine.shape[1]
    hits = jnp.where(iota((16, count), 0) == slot, 1.0, 0.0)
    before = jnp.where(iota((count, count), 0) < iota((count, count), 1), 1.0, 0.0).astype(BF16)
    position = jnp.sum(hits * dot(hits.astype(BF16), before), axis=0, keepdims=True)
    row = iota((8, count), 0)
    facts = jnp.ones((8, count), jnp.int32)
    for index, entry in enumerate((fine >> 7, fine & 127, face, coarse >> 7, coarse & 127, cface, sub)):
        facts = jnp.where(row == index, entry, facts)
    facts = facts.astype(F32)
    stacked = jnp.concatenate([facts * hits[k : k + 1] for k in range(9)], axis=0).astype(BF16)
    packed = dot_nt(stacked, one_hot(EB, position))
    for k in range(9):
        own_m[k] = packed[8 * k : 8 * k + 8]
    scale = jnp.where(level == 0, 1.0, jnp.where(level == 1, 0.5, 0.25))

    def faces_of(t, field):
        pick = pick_ref[...]
        field_h, field_l = split(field)
        f_h = dot(pick, field_h)
        f_l = dot(pick, field_l)
        faces = f_h + f_l
        own_x[t, 0] = faces[:, 0:EB]
        own_x[t, 1] = faces[:, (EA - 1) * EB :]
        f_h = f_h.astype(BF16)
        f_l = f_l.astype(BF16)
        edges = dot(f_h, edge_ref[...]) + dot(f_l, edge_ref[...])
        own = None
        for f in range(6):
            part = jnp.where(lane_face == f, edges[f * FR : (f + 1) * FR], 0.0)
            own = part if own is None else own + part
        own_y[t] = own
        return field_h, field_l, f_h, f_l, faces, own

    def send(t):
        for index in (2, 3, 4, 5, 0, 1):
            if_there(EDGE_DIRS[index], lambda: y_copy(t, index, False).start())
        for side in range(2):
            if_there((1, 7)[side], lambda: x_copy(t, side, False).start())

    for load in loads[7:10]:
        load.wait()
    views = faces_of(0, b_ref[...])

    pl.semaphore_wait(barrier, expected)
    send(0)
    for d in (0, 2, 6, 8, 3, 5, 1, 7):
        if_there(d, lambda: m_copy(d, False).start())

    for load in loads[10:]:
        load.wait()
    for d in range(3):
        high, low = split(stiff_ref[d])
        stiff_h[d] = high
        stiff_l[d] = low
    proj_s[...] = jnp.zeros_like(proj_s)
    proj_c[...] = jnp.zeros_like(proj_c)
    for s in range(4):
        table = proj_ref[:, s, :]
        proj_s[s * FR : s * FR + SIDE, 0:SIDE] = table
        proj_c[0:SIDE, s * FR : s * FR + SIDE] = table
    proj_t[...] = proj_s[...].T[0:FR]
    proj_s_h, proj_s_l = split(proj_s[0 : 4 * FR, 0:FR])
    proj_c_h, proj_c_l = split(proj_c[:, 0 : 4 * FR])
    proj_t_h, proj_t_l = split(proj_t[:, 0 : 4 * FR])

    me = own_m[4]
    self_fine = code(me[0:1] * float(EB) + me[1:2], me[7:8])
    self_coarse = code(me[3:4] * float(EB) + me[4:5], me[7:8])
    oh_self[...] = one_hot(ELEMS, jnp.concatenate([self_fine, self_coarse], axis=1))

    def edge_codes(held):
        parts_f, parts_c = [], []
        for d in EDGE_DIRS:
            facts_d = held[d]
            pair = facts_d[0:1] + float(EDGE_BASE[d]) if d in (3, 5) else float(EDGE_BASE[d])
            parts_f.append(code(facts_d[2:3] * 16.0 + pair, facts_d[7:8]))
            parts_c.append(code(facts_d[6:7] * 128.0 + facts_d[5:6] * 16.0 + pair, facts_d[7:8]))
        return (
            one_hot(128, jnp.concatenate(parts_f, axis=1)),
            one_hot(512, jnp.concatenate(parts_c, axis=1)),
        )

    ones = jnp.ones((16, 6 * EB), BF16)
    edge_f, edge_c = edge_codes(own_m)
    n_out[...] = dot_nt(edge_f, edge_c).astype(BF16)
    sum_out = dot_nt(ones, edge_f)[0:1]

    def mortar_jump(coarses, fines, subs):
        high = coarses.astype(BF16).astype(F32)
        return by_table(proj_c_h, proj_c_l, by_subface(high, subs), by_subface(coarses - high, subs)) - fines

    def mortar_back(jump, subs):
        high = jump.astype(BF16).astype(F32)
        return by_table(proj_t_h, proj_t_l, by_subface(high, subs), by_subface(jump - high, subs))

    def local_part(field, views):
        field_h, field_l, f_h, f_l, faces, own = views
        got = dot(f_h, oh_self[...]) + dot(f_l, oh_self[...])
        jump = mortar_jump(pick_face(got[:, EB:], me[5:6]), pick_face(got[:, 0:EB], me[2:3]), me[6:7])
        back = mortar_back(jump, me[6:7])
        terms = jnp.concatenate([-PENALTY * jump, PENALTY * back], axis=1)
        s_h, s_l = spread_split(terms, jnp.concatenate([me[2:3], me[5:6]], axis=1))
        gathered = dot_nt(s_h, oh_self[...]) + dot_nt(s_l, oh_self[...])

        blocks = []
        for a in range(EA):
            here = slice(a * EB, (a + 1) * EB)
            x_low, x_high = faces[0:FR, here], faces[FR : 2 * FR, here]
            y_low, y_high = faces[2 * FR : 3 * FR, here], faces[3 * FR : 4 * FR, here]
            left = x_low if a == 0 else x_low - faces[FR : 2 * FR, (a - 1) * EB : a * EB]
            right = x_high if a == EA - 1 else x_high - faces[0:FR, (a + 1) * EB : (a + 2) * EB]
            below = jnp.where(lane == 0, 0.0, pltpu.roll(y_high, 1, 1))
            above = jnp.where(lane == EB - 1, 0.0, pltpu.roll(y_low, EB - 1, 1))
            lateral = jnp.concatenate([left, right, y_low - below, y_high - above], axis=0)
            blocks.append(jnp.concatenate([PENALTY * lateral, jnp.zeros((2 * FR, EB), F32)], axis=0))
        gathered = gathered + jnp.concatenate(blocks, axis=1)

        total = field
        for d in range(3):
            total = total + metric_ref[d : d + 1, :] * by_table(stiff_h[d], stiff_l[d], field_h, field_l)
        return scale * total, gathered

    def remote_part(t, views, gathered, sum_in):
        field_h, field_l, f_h, f_l, faces, own = views
        fines, coarses, subs = [], [], []
        for side in range(2):
            d = (1, 7)[side]
            here = slice(0, EB) if side == 0 else slice((EA - 1) * EB, EA * EB)
            h_h, h_l = split(halo_x[t, side])
            got = dot(jnp.concatenate([f_h[:, here], h_h], axis=0), oh_x[side])
            got = got + dot(jnp.concatenate([f_l[:, here], h_l], axis=0), oh_x[side])
            ours, theirs = got[0:FACES], got[FACES:]
            fines += [pick_face(ours[:, 0:EB], own_m[d][2:3]), pick_face(theirs[:, EB:], halo_m[d][2:3])]
            coarses += [pick_face(theirs[:, 0:EB], own_m[d][5:6]), pick_face(ours[:, EB:], halo_m[d][5:6])]
            subs += [own_m[d][6:7], halo_m[d][6:7]]
        jump = mortar_jump(*(jnp.concatenate(parts, axis=1) for parts in (coarses, fines, subs)))
        jump = [jump[:, k * EB : (k + 1) * EB] for k in range(4)]
        back = mortar_back(jnp.concatenate([jump[1], jump[3]], axis=1), jnp.concatenate([subs[1], subs[3]], axis=1))
        side_terms = []
        for side in range(2):
            d = (1, 7)[side]
            terms = jnp.concatenate(
                [-PENALTY * jump[2 * side], PENALTY * back[:, side * EB : (side + 1) * EB]], axis=1
            )
            s_h, s_l = spread_split(terms, jnp.concatenate([own_m[d][2:3], halo_m[d][5:6]], axis=1))
            side_term = dot_nt(s_h, oh_x[side]) + dot_nt(s_l, oh_x[side])
            if side == 0:
                beside = [-PENALTY * halo_x[t, 0, FR : 2 * FR, :], jnp.zeros((5 * FR, EB), F32)]
            else:
                beside = [jnp.zeros((FR, EB), F32), -PENALTY * halo_x[t, 1, 0:FR, :], jnp.zeros((4 * FR, EB), F32)]
            side_terms.append(side_term + jnp.concatenate(beside, axis=0))

        across = jnp.zeros((FR, 128), F32)
        for index, (d, turn, low, high) in enumerate(
            ((3, -4, 0, 4), (5, 4, 4, 8), (0, -3, 8, 9), (2, -1, 9, 10), (6, 1, 10, 11), (8, 3, 11, 12))
        ):
            moved = pltpu.roll(halo_y[t, index], turn % 128, 1)
            across = jnp.where((lane_pair >= low) & (lane_pair < high), moved, across)
        pairs = jnp.concatenate([own, across], axis=1)
        pairs_h, pairs_l = split(pairs)
        images = by_table(proj_s_h, proj_s_l, pairs_h, pairs_l)
        image_own = jnp.concatenate([images[s * FR : (s + 1) * FR, 0:128] for s in range(4)], axis=1)
        image_far = jnp.concatenate([images[s * FR : (s + 1) * FR, 128:] for s in range(4)], axis=1)
        far_h, far_l = split(image_far)
        on_fine = own * sum_out - dot_nt(far_h, n_out[...]) - dot_nt(far_l, n_out[...])
        jumps = image_own * sum_in - dot(pairs_h[:, 128:], n_in[...]) - dot(pairs_l[:, 128:], n_in[...])
        jumps = jnp.concatenate([jumps[:, s * 128 : (s + 1) * 128] for s in range(4)], axis=0)
        jumps_h, jumps_l = split(jumps)
        on_edge = PENALTY * (on_fine + by_table(proj_t_h, proj_t_l, jumps_h, jumps_l))
        from_low = pltpu.roll(across, 128 - 16, 1)
        from_high = pltpu.roll(across, 16, 1)
        on_edge = on_edge - PENALTY * jnp.where(
            (lane_face == 2) & (lane_pair < 4),
            from_low,
            jnp.where((lane_face == 3) & (lane_pair >= 4) & (lane_pair < 8), from_high, 0.0),
        )
        e_high = on_edge.astype(BF16).astype(F32)
        e_low = on_edge - e_high
        e_h = jnp.concatenate([jnp.where(lane_face == f, e_high, 0.0) for f in range(6)], axis=0).astype(BF16)
        e_l = jnp.concatenate([jnp.where(lane_face == f, e_low, 0.0) for f in range(6)], axis=0).astype(BF16)
        gathered = gathered + dot_nt(e_h, edge_ref[...]) + dot_nt(e_l, edge_ref[...])

        middle = jnp.zeros((FACES, (EA - 2) * EB), F32)
        gathered = gathered + jnp.concatenate([side_terms[0], middle, side_terms[1]], axis=1)
        g_h, g_l = split(gathered)
        place = place_ref[...]
        return dot(place, g_h) + dot(place, g_l)

    def arrive(t):
        for side in range(2):
            if_there((1, 7)[side], lambda: x_copy(t, side, True).wait_recv())
        for index in range(6):
            if_there(EDGE_DIRS[index], lambda: y_copy(t, index, True).wait_recv())

    b = b_ref[...]
    total, gathered = local_part(b, views)
    for d in DIRS:
        if_there(d, lambda: m_copy(d, True).wait_recv())
    for side in range(2):
        d = (1, 7)[side]
        both = jnp.concatenate([own_m[d], halo_m[d]], axis=1)
        oh_x[side] = one_hot(EB, code(both[1:2], both[7:8]))
    edge_f, edge_c = edge_codes(halo_m)
    n_in[...] = dot_nt(edge_f, edge_c).astype(BF16)
    sum_in = dot_nt(ones, edge_c)[0:1]
    arrive(0)
    q = total + remote_part(0, views, gathered, sum_in)

    views = faces_of(1, q)
    send(1)
    q_ref[...] = q
    total, gathered = local_part(q, views)
    b = b_ref[...]
    q = q_ref[...]
    early = [column_sums(b, b), column_sums(b, q), column_sums(q, q)]
    arrive(1)
    w = total + remote_part(1, views, gathered, sum_in)
    w_ref[...] = w
    early += [column_sums(b_ref[...], w), column_sums(q_ref[...], w)]

    lanes = jnp.zeros((1, 128), F32)
    for index, sums in enumerate(early):
        lanes = jnp.where(lane == index, jnp.sum(sums, axis=1, keepdims=True), lanes)
    mine0[...] = lanes
    core = pltpu.make_async_remote_copy(
        src_ref=mine0,
        dst_ref=red0,
        send_sem=s0_send,
        recv_sem=s0_recv,
        device_id={"gx": gx + 1 - 2 * lax.rem(gx, 2), "gy": gy},
        device_id_type=MESH,
    )
    core.start()
    core.wait_recv()
    lanes = mine0[...] + red0[...]
    mine1[...] = lanes
    for k, offset in enumerate(chips):
        pltpu.make_async_remote_copy(
            src_ref=mine1,
            dst_ref=red1.at[k],
            send_sem=s1_send,
            recv_sem=s1_recv,
            device_id=chip(offset),
            device_id_type=MESH,
        ).start()
    pltpu.make_async_copy(red1, red1, s1_recv).wait()
    lanes = lanes + jnp.sum(red1[...], axis=0)

    bb, bq, qq, bw, qw = (lanes[:, i : i + 1] for i in range(5))
    alpha = bb / bq
    new = bb - 2.0 * alpha * bq + alpha * alpha * qq
    grow = 1.0 + new / bb
    alpha_next = new / (grow * grow * bq - grow * alpha * (bw + qq) + alpha * alpha * qw)
    row = iota((8, ELEMS), 0)
    coef_ref[...] = jnp.where(row == 0, alpha + alpha_next * grow, alpha * alpha_next)

    for t in range(2):
        for side in range(2):
            if_there((1, 7)[side], lambda: x_copy(t, side, False).wait_send())
        for index in range(6):
            if_there(EDGE_DIRS[index], lambda: y_copy(t, index, False).wait_send())
    for d in DIRS:
        if_there(d, lambda: m_copy(d, False).wait_send())
    core.wait_send()
    pltpu.make_async_copy(red1, red1, s1_send).wait()


def body(
    n_gx,
    n_gy,
    right_side,
    stiffness,
    metric,
    levels,
    projection,
    mortar_fine,
    mortar_face,
    mortar_owner,
    mortar_subface,
    mortar_coarse,
    mortar_cface,
):
    pick, place, edge = (jnp.asarray(table, BF16) for table in constant_tables())
    field = jax.ShapeDtypeStruct(right_side.shape, F32)
    count = mortar_fine.shape[0]
    others = n_gx // 2 * n_gy - 1
    hbm = pl.BlockSpec(memory_space=pltpu.HBM)
    vmem = pl.BlockSpec(memory_space=pltpu.VMEM)
    dma = pltpu.SemaphoreType.DMA
    line = [
        entry.reshape(1, count)
        for entry in (
            mortar_fine,
            mortar_face,
            mortar_owner,
            mortar_subface,
            mortar_coarse,
            mortar_cface,
            levels,
        )
    ]
    q, w, coef = pl.pallas_call(
        functools.partial(kernel, n_gx, n_gy),
        out_shape=(field, field, jax.ShapeDtypeStruct((8, ELEMS), F32)),
        in_specs=[hbm] * 14,
        out_specs=(vmem, vmem, vmem),
        scratch_shapes=[
            pltpu.VMEM((NODES, ELEMS), F32),
            pltpu.VMEM((3, NODES, NODES), F32),
            pltpu.VMEM((3, ELEMS), F32),
            pltpu.VMEM((7, 1, ELEMS), jnp.int32),
            pltpu.VMEM((SIDE, 4, SIDE), F32),
            pltpu.VMEM((FACES, NODES), BF16),
            pltpu.VMEM((NODES, FACES), BF16),
            pltpu.VMEM((ELEMS, 128), BF16),
            pltpu.VMEM((2, 2, FACES, EB), F32),
            pltpu.VMEM((2, 6, FR, 128), F32),
            pltpu.VMEM((9, 8, 128), F32),
            pltpu.VMEM((9, 8, 128), F32),
            pltpu.VMEM((2, 2, FACES, EB), F32),
            pltpu.VMEM((2, FR, 128), F32),
            pltpu.VMEM((3, NODES, NODES), BF16),
            pltpu.VMEM((3, NODES, NODES), BF16),
            pltpu.VMEM((ELEMS, 2 * EB), BF16),
            pltpu.VMEM((2, EB, 2 * EB), BF16),
            pltpu.VMEM((128, 512), BF16),
            pltpu.VMEM((128, 512), BF16),
            pltpu.VMEM((256, 128), F32),
            pltpu.VMEM((FR, 256), F32),
            pltpu.VMEM((FR, 256), F32),
            pltpu.VMEM((1, 128), F32),
            pltpu.VMEM((others, 1, 128), F32),
            pltpu.VMEM((1, 128), F32),
            pltpu.VMEM((1, 128), F32),
            dma((14,)),
            dma((2, 2)),
            dma((2, 2)),
            dma((2, 6)),
            dma((2, 6)),
            dma((9,)),
            dma((9,)),
            dma,
            dma,
            dma,
            dma,
        ],
        compiler_params=pltpu.CompilerParams(
            collective_id=0, has_side_effects=True, vmem_limit_bytes=48 * 1024 * 1024
        ),
    )(right_side, stiffness, metric, *line, projection.transpose(1, 0, 2), pick, place, edge)
    first, second = coef[0:1], coef[1:2]
    return first * right_side - second * q, right_side - first * q + second * w


def solution(mesh):
    columns = P(None, ("gx", "gy"))
    faces = P(("gx", "gy"))
    in_specs = (columns, P(), columns, faces, P(), faces, faces, P(("gx", "gy"), None), faces, faces, faces)
    run = functools.partial(body, mesh.shape["gx"], mesh.shape["gy"])
    return jax.shard_map(run, mesh=mesh, in_specs=in_specs, out_specs=(columns, columns), check_vma=False)
```

time: 41.4 us -> 42.5 us (1.027)
  Pallas kernels: 33.3 us -> 31.2 us
  local copies, waits for them, and re-layouts: 7.19 us -> 9.11 us
  other arithmetic: 0 us -> 1.06 us
    unnamed x15 -> x28, local copies, waits for them, and re-layouts: 6.33 us -> 9.11 us
    pallas_call x1, Pallas kernels: 33.3 us -> 31.2 us  [body(): pl.pallas_call(functools.partial(kernel, n_gx, n_gy), out_shape=(field, f...]
    add x0 -> x1, other arithmetic: none -> 1.06 us  [body(): right_side - first * q + second * w]
    another operation x2 -> x0, local copies, waits for them, and re-layouts: 0.86 us -> none  [body(): jnp.stack([mortar_fine, mortar_face, mortar_owner[:, 0], mortar_subface,...]
where the time goes in v1:
time: 42.5 us; the launch traced here: 42.1 us
  Pallas kernels  31.2 us (73%)
  local copies, waits for them, and re-layouts  9.11 us (21%)
  other arithmetic  1.06 us (2%)
  between operations  0.69 us (2%)
    pallas_call x1, Pallas kernels, body(): pl.pallas_call(functools.partial(kernel, n_gx, n_gy), out_shape=(field, f...  31.2 us
    unnamed x28, local copies, waits for them, and re-layouts  9.11 us
    add x1, other arithmetic, body(): right_side - first * q + second * w  1.06 us

profile of v1, /device:TPU:1, one launch (start us, length us, event | category | flops | bytes accessed | tf_op | source)
XLA Modules:
  0.0 42.1 jit_solution(6882050998903286049)
XLA Ops:
  0.6 0.0 copy-start.6
  0.6 0.0 copy-start.9
  0.7 0.0 copy-start.8
  0.7 0.0 copy-start.7
  0.7 0.7 %copy-done.6 = f32[3,512]{1,0:T(4,128)S(1)} copy-done((f32[3,512]{1,0:T(4,128)S(1)}, f32[3,512]{1,0:T(4,128)}, u32[]{:S(2)}) %copy-start.6) | copy-done | bytes 6168
  1.3 0.0 copy-done.9
  1.3 0.0 copy-done.8
  1.3 0.0 copy-done.7
  1.4 0.0 copy-start
  1.4 1.0 %copy-done = f32[216,512]{1,0:T(8,128)S(1)} copy-done((f32[216,512]{1,0:T(8,128)S(1)}, f32[216,512]{1,0:T(8,128)}, u32[]{:S(2)}) %copy-start) | copy-done | bytes 442392
  2.4 0.0 copy-start.1
  2.4 1.1 %copy-done.1 = f32[3,216,216]{2,1,0:T(8,128)S(1)} copy-done((f32[3,216,216]{2,1,0:T(8,128)S(1)}, f32[3,216,216]{2,1,0:T(8,128)}, u32[]{:S(2)}) %copy-start.1) | copy-done | bytes 559896
  3.5 0.0 copy-start.2
  3.5 0.9 %copy-done.2 = bf16[512,128]{1,0:T(8,128)(2,1)S(1)} copy-done((bf16[512,128]{1,0:T(8,128)(2,1)S(1)}, bf16[512,128]{1,0:T(8,128)(2,1)}, u32[]{:S(2)}) %copy-start.2) | copy-done | bytes 131096
  4.4 0.0 copy-start.3
  4.4 0.9 %copy-done.3 = bf16[240,216]{1,0:T(8,128)(2,1)S(1)} copy-done((bf16[240,216]{1,0:T(8,128)(2,1)S(1)}, bf16[240,216]{1,0:T(8,128)(2,1)}, u32[]{:S(2)}) %copy-start.3) | copy-done | bytes 103704
  5.3 0.0 copy-start.4
  5.3 0.9 %copy-done.4 = bf16[216,240]{1,0:T(8,128)(2,1)S(1)} copy-done((bf16[216,240]{1,0:T(8,128)(2,1)S(1)}, bf16[216,240]{1,0:T(8,128)(2,1)}, u32[]{:S(2)}) %copy-start.4) | copy-done | bytes 103704
  6.2 0.0 copy-start.5
  6.2 0.9 %copy-done.5 = f32[4,36,36]{2,0,1:T(4,128)S(1)} copy-done((f32[4,36,36]{2,0,1:T(4,128)S(1)}, f32[4,36,36]{2,0,1:T(4,128)}, u32[]{:S(2)}) %copy-start.5) | copy-done | bytes 20760
  7.1 0.0 copy-start.10
  7.1 0.7 %copy-done.10 = s32[512]{0:T(512)S(1)} copy-done((s32[512]{0:T(512)S(1)}, s32[512]{0:T(512)}, u32[]{:S(2)}) %copy-start.10) | copy-done | bytes 2072
  7.7 0.0 copy-start.11
  7.7 0.7 %copy-done.11 = s32[512]{0:T(512)S(1)} copy-done((s32[512]{0:T(512)S(1)}, s32[512]{0:T(512)}, u32[]{:S(2)}) %copy-start.11) | copy-done | bytes 2072
  8.4 0.0 copy-start.12
  8.4 0.7 %copy-done.12 = s32[512]{0:T(512)S(1)} copy-done((s32[512]{0:T(512)S(1)}, s32[512]{0:T(512)}, u32[]{:S(2)}) %copy-start.12) | copy-done | bytes 2072
  9.1 0.0 copy-start.13
  9.1 0.7 %copy-done.13 = s32[512]{0:T(512)S(1)} copy-done((s32[512]{0:T(512)S(1)}, s32[512]{0:T(512)}, u32[]{:S(2)}) %copy-start.13) | copy-done | bytes 2072
  9.8 31.2 %shard_map.149 = (f32[216,512]{1,0:T(8,128)S(1)}, f32[216,512]{1,0:T(8,128)S(1)}, f32[8,512]{1,0:T(8,128)S(1)}) custom-call(f32[216,512]{1,0:T(8,128)S(1)} %copy-done, f32[3,216,216]{2,1,0:T(8,128)S(1)} %copy-done.1, f32[3,512]{1,0:T(4,128)S(1)} %copy-done.6, s32[1,512]{1,0:T(1,128)S(1)} %bitcast.11, s32[1,512]{1,0:T(1,128)S(1)} %bitcast.12, ...), custom_call_target="tpu_custom_call" | custom-call | tf_op jit(solution)/shard_map/pallas_call | solution.py:552
  41.0 1.1 %multiply_add_fusion = (f32[216,512]{1,0:T(8,128)}, f32[216,512]{1,0:T(8,128)}) fusion(f32[216,512]{1,0:T(8,128)S(1)} %get-tuple-element.7, f32[216,512]{1,0:T(8,128)S(1)} %copy-done, f32[216,512]{1,0:T(8,128)S(1)} %get-tuple-element.6, f32[512]{0:T(512)S(1)} %bitcast.19, f32[512]{0:T(512)S(1)} %bitcast.18), kind=kLoop, calls=%fused_computation | loop fusion | flops 774144 | bytes 2215936 | tf_op jit(solution)/shard_map/add | solution.py:602
  (1 shorter events, 0.0 us)
Async XLA Ops:
  0.6 0.7 %copy-start.6 = (f32[3,512]{1,0:T(4,128)S(1)}, f32[3,512]{1,0:T(4,128)}, u32[]{:S(2)}) copy-start(f32[3,512]{1,0:T(4,128)} %metric_hbm.1) | copy-start | bytes 18436
  0.6 0.7 %copy-start.9 = (s32[512,1]{0,1:T(1,128)S(1)}, s32[512,1]{0,1:T(1,128)}, u32[]{:S(2)}) copy-start(s32[512,1]{0,1:T(1,128)} %param.21) | copy-start | bytes 6148
  0.7 0.7 %copy-start.8 = (s32[512]{0:T(512)S(1)}, s32[512]{0:T(512)}, u32[]{:S(2)}) copy-start(s32[512]{0:T(512)} %param.20) | copy-start | bytes 6148
  0.7 0.7 %copy-start.7 = (s32[512]{0:T(512)S(1)}, s32[512]{0:T(512)}, u32[]{:S(2)}) copy-start(s32[512]{0:T(512)} %param.19) | copy-start | bytes 6148
  1.4 1.0 %copy-start = (f32[216,512]{1,0:T(8,128)S(1)}, f32[216,512]{1,0:T(8,128)}, u32[]{:S(2)}) copy-start(f32[216,512]{1,0:T(8,128)} %b_hbm.1) | copy-start | bytes 1327108
  2.4 1.1 %copy-start.1 = (f32[3,216,216]{2,1,0:T(8,128)S(1)}, f32[3,216,216]{2,1,0:T(8,128)}, u32[]{:S(2)}) copy-start(f32[3,216,216]{2,1,0:T(8,128)} %stiff_hbm.1) | copy-start | bytes 1679620
  3.5 0.9 %copy-start.2 = (bf16[512,128]{1,0:T(8,128)(2,1)S(1)}, bf16[512,128]{1,0:T(8,128)(2,1)}, u32[]{:S(2)}) copy-start(bf16[512,128]{1,0:T(8,128)(2,1)} %constant.8.clone.edge_hbm) | copy-start | bytes 393220
  4.4 0.9 %copy-start.3 = (bf16[240,216]{1,0:T(8,128)(2,1)S(1)}, bf16[240,216]{1,0:T(8,128)(2,1)}, u32[]{:S(2)}) copy-start(bf16[240,216]{1,0:T(8,128)(2,1)} %constant.6.clone.pick_hbm) | copy-start | bytes 311044
  5.3 0.9 %copy-start.4 = (bf16[216,240]{1,0:T(8,128)(2,1)S(1)}, bf16[216,240]{1,0:T(8,128)(2,1)}, u32[]{:S(2)}) copy-start(bf16[216,240]{1,0:T(8,128)(2,1)} %constant.7.clone.place_hbm) | copy-start | bytes 311044
  6.2 0.9 %copy-start.5 = (f32[4,36,36]{2,0,1:T(4,128)S(1)}, f32[4,36,36]{2,0,1:T(4,128)}, u32[]{:S(2)}) copy-start(f32[4,36,36]{2,0,1:T(4,128)} %param.18) | copy-start | bytes 62212
  7.1 0.7 %copy-start.10 = (s32[512]{0:T(512)S(1)}, s32[512]{0:T(512)}, u32[]{:S(2)}) copy-start(s32[512]{0:T(512)} %param.22) | copy-start | bytes 6148
  7.7 0.7 %copy-start.11 = (s32[512]{0:T(512)S(1)}, s32[512]{0:T(512)}, u32[]{:S(2)}) copy-start(s32[512]{0:T(512)} %param.23) | copy-start | bytes 6148
  8.4 0.7 %copy-start.12 = (s32[512]{0:T(512)S(1)}, s32[512]{0:T(512)}, u32[]{:S(2)}) copy-start(s32[512]{0:T(512)} %param.24) | copy-start | bytes 6148
  9.1 0.7 %copy-start.13 = (s32[512]{0:T(512)S(1)}, s32[512]{0:T(512)}, u32[]{:S(2)}) copy-start(s32[512]{0:T(512)} %param.17) | copy-start | bytes 6148

commit v2 on v1

--- a/solution.py
+++ b/solution.py
@@ -165,7 +165,7 @@
 
     size_x, size_y, size_z = n_gx // 2, n_gy // 4, 4
     chips = [(i, j, k) for i in range(size_x) for j in range(size_y) for k in range(size_z)][1:]
-    chips.sort(key=lambda c: -sum(min(v, n - v) for v, n in zip(c, (size_x, size_y, size_z))))
+    chips.sort(key=lambda c: sum((v - 1) % n for v, n in zip(c, (size_x, size_y, size_z))))
 
     def chip(offset):
         y, z = gy // size_z, lax.rem(gy, size_z)
@@ -372,6 +372,8 @@
 
     def remote_part(t, views, gathered, sum_in):
         field_h, field_l, f_h, f_l, faces, own = views
+        for side in range(2):
+            if_there((1, 7)[side], lambda: x_copy(t, side, True).wait_recv())
         fines, coarses, subs = [], [], []
         for side in range(2):
             d = (1, 7)[side]
@@ -400,6 +402,8 @@
                 beside = [jnp.zeros((FR, EB), F32), -PENALTY * halo_x[t, 1, 0:FR, :], jnp.zeros((4 * FR, EB), F32)]
             side_terms.append(side_term + jnp.concatenate(beside, axis=0))
 
+        for index in range(6):
+            if_there(EDGE_DIRS[index], lambda: y_copy(t, index, True).wait_recv())
         across = jnp.zeros((FR, 128), F32)
         for index, (d, turn, low, high) in enumerate(
             ((3, -4, 0, 4), (5, 4, 4, 8), (0, -3, 8, 9), (2, -1, 9, 10), (6, 1, 10, 11), (8, 3, 11, 12))
@@ -436,12 +440,6 @@
         place = place_ref[...]
         return dot(place, g_h) + dot(place, g_l)
 
-    def arrive(t):
-        for side in range(2):
-            if_there((1, 7)[side], lambda: x_copy(t, side, True).wait_recv())
-        for index in range(6):
-            if_there(EDGE_DIRS[index], lambda: y_copy(t, index, True).wait_recv())
-
     b = b_ref[...]
     total, gathered = local_part(b, views)
     for d in DIRS:
@@ -453,7 +451,6 @@
     edge_f, edge_c = edge_codes(halo_m)
     n_in[...] = dot_nt(edge_f, edge_c).astype(BF16)
     sum_in = dot_nt(ones, edge_c)[0:1]
-    arrive(0)
     q = total + remote_part(0, views, gathered, sum_in)
 
     views = faces_of(1, q)
@@ -463,7 +460,6 @@
     b = b_ref[...]
     q = q_ref[...]
     early = [column_sums(b, b), column_sums(b, q), column_sums(q, q)]
-    arrive(1)
     w = total + remote_part(1, views, gathered, sum_in)
     w_ref[...] = w
     early += [column_sums(b_ref[...], w), column_sums(q_ref[...], w)]
@@ -501,7 +497,7 @@
     new = bb - 2.0 * alpha * bq + alpha * alpha * qq
     grow = 1.0 + new / bb
     alpha_next = new / (grow * grow * bq - grow * alpha * (bw + qq) + alpha * alpha * qw)
-    row = iota((8, ELEMS), 0)
+    row = iota((8, 128), 0)
     coef_ref[...] = jnp.where(row == 0, alpha + alpha_next * grow, alpha * alpha_next)
 
     for t in range(2):
@@ -513,6 +509,22 @@
         if_there(d, lambda: m_copy(d, False).wait_send())
     core.wait_send()
     pltpu.make_async_copy(red1, red1, s1_send).wait()
+
+
+def finish(coef_ref, b_ref, q_ref, w_ref, x_hbm, r_hbm, made, out_sem):
+    first, second = coef_ref[0:1, 0:1], coef_ref[1:2, 0:1]
+    stores = []
+    for part, (start, size) in enumerate(((0, 104), (104, NODES - 104))):
+        rows = pl.ds(start, size)
+        b, q, w = b_ref[rows, :], q_ref[rows, :], w_ref[rows, :]
+        made[0, rows, :] = first * b - second * q
+        made[1, rows, :] = b - first * q + second * w
+        for k, target in enumerate((x_hbm, r_hbm)):
+            store = pltpu.make_async_copy(made.at[k, rows], target.at[rows], out_sem.at[part, k])
+            store.start()
+            stores.append(store)
+    for store in stores:
+        store.wait()
 
 
 def body(
@@ -551,7 +563,7 @@
     ]
     q, w, coef = pl.pallas_call(
         functools.partial(kernel, n_gx, n_gy),
-        out_shape=(field, field, jax.ShapeDtypeStruct((8, ELEMS), F32)),
+        out_shape=(field, field, jax.ShapeDtypeStruct((8, 128), F32)),
         in_specs=[hbm] * 14,
         out_specs=(vmem, vmem, vmem),
         scratch_shapes=[
@@ -595,11 +607,22 @@
             dma,
         ],
         compiler_params=pltpu.CompilerParams(
-            collective_id=0, has_side_effects=True, vmem_limit_bytes=48 * 1024 * 1024
+            collective_id=0, has_side_effects=True, vmem_limit_bytes=40 * 1024 * 1024
         ),
-    )(right_side, stiffness, metric, *line, projection.transpose(1, 0, 2), pick, place, edge)
-    first, second = coef[0:1], coef[1:2]
-    return first * right_side - second * q, right_side - first * q + second * w
+    )(
+        *(
+            pltpu.with_memory_space_constraint(operand, pltpu.HBM)
+            for operand in (right_side, stiffness, metric, *line, projection.transpose(1, 0, 2), pick, place, edge)
+        )
+    )
+    return pl.pallas_call(
+        finish,
+        out_shape=(field, field),
+        in_specs=[vmem] * 4,
+        out_specs=(hbm, hbm),
+        scratch_shapes=[pltpu.VMEM((2, NODES, ELEMS), F32), dma((2, 2))],
+        compiler_params=pltpu.CompilerParams(vmem_limit_bytes=40 * 1024 * 1024),
+    )(coef, right_side, q, w)
 
 
 def solution(mesh):

time: 42.5 us -> 33.5 us (0.79)
  local copies, waits for them, and re-layouts: 9.11 us -> 0.01 us
  Pallas kernels: 31.2 us -> 32.7 us
  other arithmetic: 1.06 us -> 0 us
    unnamed x28 -> x2, local copies, waits for them, and re-layouts: 9.11 us -> 0.01 us
    pallas_call x0 -> x1, Pallas kernels: none -> 1.08 us  [body(): pl.pallas_call(finish, out_shape=(field, field), in_specs=[vmem] * 4, out...]
    add x1 -> x0, other arithmetic: 1.06 us -> none  [body(): right_side - first * q + second * w]
    pallas_call x1, Pallas kernels: 31.2 us -> 31.6 us  [body(): pl.pallas_call(functools.partial(kernel, n_gx, n_gy), out_shape=(field, f...]
where the time goes in v2:
time: 33.5 us; the launch traced here: 33.4 us
  Pallas kernels  32.7 us (98%)
  between operations  0.66 us (2%)
    pallas_call x1, Pallas kernels, body(): pl.pallas_call(functools.partial(kernel, n_gx, n_gy), out_shape=(field, f...  31.6 us
    pallas_call x1, Pallas kernels, body(): pl.pallas_call(finish, out_shape=(field, field), in_specs=[vmem] * 4, out...  1.08 us

profile of v2, /device:TPU:1, one launch (start us, length us, event | category | flops | bytes accessed | tf_op | source)
XLA Modules:
  0.0 33.4 jit_solution(7475166060548969550)
XLA Ops:
  0.6 0.0 copy-start
  0.6 31.6 %shard_map.149 = (f32[216,512]{1,0:T(8,128)S(1)}, f32[216,512]{1,0:T(8,128)S(1)}, f32[8,128]{1,0:T(8,128)S(1)}) custom-call(f32[216,512]{1,0:T(8,128)} %b_ref.1, f32[3,216,216]{2,1,0:T(8,128)} %stiff_hbm.1, f32[3,512]{1,0:T(4,128)} %metric_hbm.1, s32[1,512]{1,0:T(1,128)} %bitcast.9, s32[1,512]{1,0:T(1,128)} %bitcast.10, s32[1,512]{1,0:T(1,128)} %bitcast.11, ...), custom_call_target="tpu_custom_call" | custom-call | tf_op jit(solution)/shard_map/pallas_call | solution.py:564
  32.3 0.0 copy-done
  32.3 1.1 %shard_map.150 = (f32[216,512]{1,0:T(8,128)}, f32[216,512]{1,0:T(8,128)}) custom-call(f32[8,128]{1,0:T(8,128)S(1)} %get-tuple-element.5.coef_ref, f32[216,512]{1,0:T(8,128)S(1)} %copy-done, f32[216,512]{1,0:T(8,128)S(1)} %get-tuple-element.6.q_ref, f32[216,512]{1,0:T(8,128)S(1)} %get-tuple-element.7.w_ref), custom_call_target="tpu_custom_call" | custom-call | tf_op jit(solution)/shard_map/pallas_call | solution.py:618
Async XLA Ops:
  0.6 31.7 %copy-start = (f32[216,512]{1,0:T(8,128)S(1)}, f32[216,512]{1,0:T(8,128)}, u32[]{:S(2)}) copy-start(f32[216,512]{1,0:T(8,128)} %b_ref.1) | copy-start | bytes 1327108

commit v3 on v2

v3 whole, which is shorter than its diff:
```python
import functools

import jax
import jax.numpy as jnp
import numpy as np
from jax import lax
from jax.experimental import pallas as pl
from jax.experimental.pallas import tpu as pltpu
from jax.sharding import PartitionSpec as P

NP = 6
NODES = NP * NP * NP
SIDE = NP * NP
EA = 4
EB = 128
ELEMS = EA * EB
FR = 40
FACES = 6 * FR
SP = 224
PENALTY = 1.0

F32 = jnp.float32
BF16 = jnp.bfloat16
MESH = pl.DeviceIdType.MESH

DIRS = {d: (d // 3 - 1, d % 3 - 1) for d in range(9) if d != 4}
EDGE_DIRS = (3, 5, 0, 2, 6, 8)
CORNERS = {0: 8, 2: 9, 6: 10, 8: 11}
CORNER_SHIFT = {8: 7, 9: 9, 10: 3, 11: 5}


def face_nodes(face):
    ids = np.arange(NODES).reshape(NP, NP, NP)
    return [ids[0], ids[5], ids[:, 0], ids[:, 5], ids[:, :, 0], ids[:, :, 5]][face].reshape(-1)


def constant_tables():
    pick = np.zeros((FACES, NODES), np.float32)
    for face in range(6):
        pick[face * FR + np.arange(SIDE), face_nodes(face)] = 1.0
    return pick, pick.T.copy(), pick @ pick.T


def dot(a, b):
    return lax.dot_general(a, b, (((1,), (0,)), ((), ())), preferred_element_type=F32)


def dot_nt(a, b):
    return lax.dot_general(a, b, (((1,), (1,)), ((), ())), preferred_element_type=F32)


def split(value):
    high = value.astype(BF16)
    return high, (value - high.astype(F32)).astype(BF16)


def iota(shape, dim):
    return lax.broadcasted_iota(jnp.int32, shape, dim)


def one_hot(rows, code):
    return jnp.where(iota((rows, code.shape[1]), 0).astype(F32) == code, 1.0, 0.0).astype(BF16)


def pick_face(sides, face):
    out = None
    for f in range(6):
        part = jnp.where(face == float(f), sides[f * FR : (f + 1) * FR], 0.0)
        out = part if out is None else out + part
    return out


def spread_face(values, face):
    return jnp.concatenate([jnp.where(face == float(f), values, 0.0) for f in range(6)], axis=0)


def spread_split(values, face):
    high = values.astype(BF16).astype(F32)
    return spread_face(high, face).astype(BF16), spread_face(values - high, face).astype(BF16)


def by_subface(values, sub):
    return jnp.concatenate([jnp.where(sub == float(s), values, 0.0) for s in range(4)], axis=0).astype(BF16)


def column_sums(a, b):
    prod = a * b
    rows = jnp.sum(prod, axis=0, keepdims=True)
    return sum(rows[:, t * EB : (t + 1) * EB] for t in range(EA))


def kernel(
    n_gx,
    n_gy,
    b_hbm,
    stiff_hbm,
    metric_hbm,
    fine_hbm,
    face_hbm,
    owner_hbm,
    sub_hbm,
    coarse_hbm,
    cface_hbm,
    level_hbm,
    proj_hbm,
    pick_hbm,
    place_hbm,
    mix_hbm,
    q_ref,
    w_ref,
    coef_ref,
    b_ref,
    stiff_ref,
    metric_ref,
    ints_ref,
    proj_ref,
    pick_ref,
    place_ref,
    mix_ref,
    halo_x,
    halo_y,
    own_m,
    own_x,
    own_y,
    stiff_s,
    oh_self,
    oh_x,
    n_out,
    n_in,
    proj_s,
    proj_c,
    proj_t,
    red0,
    red1,
    mine0,
    mine1,
    in_sem,
    sx_send,
    sx_recv,
    sy_send,
    sy_recv,
    s0_send,
    s0_recv,
    s1_send,
    s1_recv,
):
    gx = lax.axis_index("gx")
    gy = lax.axis_index("gy")

    int_names = (fine_hbm, face_hbm, owner_hbm, sub_hbm, coarse_hbm, cface_hbm, level_hbm)
    loads = [(source, ints_ref.at[k]) for k, source in enumerate(int_names)]
    loads += [(b_hbm, b_ref), (pick_hbm, pick_ref), (proj_hbm, proj_ref), (mix_hbm, mix_ref)]
    loads += [(stiff_hbm, stiff_ref), (metric_hbm, metric_ref), (place_hbm, place_ref)]
    loads = [pltpu.make_async_copy(source, target, in_sem.at[k]) for k, (source, target) in enumerate(loads)]
    for load in loads:
        load.start()

    def there(d):
        dx, dy = DIRS[d]
        ok = (gx + dx >= 0) & (gx + dx < n_gx) & (gy + dy >= 0) & (gy + dy < n_gy)
        return ok, {"gx": gx + dx, "gy": gy + dy}

    def if_there(d, act):
        pl.when(there(d)[0])(act)

    size_x, size_y, size_z = n_gx // 2, n_gy // 4, 4
    chips = [(i, j, k) for i in range(size_x) for j in range(size_y) for k in range(size_z)][1:]
    chips.sort(key=lambda c: sum((v - 1) % n for v, n in zip(c, (size_x, size_y, size_z))))

    def chip(offset):
        y, z = gy // size_z, lax.rem(gy, size_z)
        return {
            "gx": lax.rem(gx + 2 * offset[0], n_gx),
            "gy": lax.rem(y + offset[1], size_y) * size_z + lax.rem(z + offset[2], size_z),
        }

    halo_x[...] = jnp.zeros_like(halo_x)
    halo_y[...] = jnp.zeros_like(halo_y)

    barrier = pltpu.get_barrier_semaphore()
    expected = jnp.int32(len(chips))
    for offset in chips:
        pl.semaphore_signal(barrier, inc=1, device_id=chip(offset), device_id_type=MESH)
    for d in (0, 2, 6, 8, 1, 7):
        ok, where = there(d)

        @pl.when(ok)
        def _():
            pl.semaphore_signal(barrier, inc=1, device_id=where, device_id_type=MESH)

        expected = expected + ok.astype(jnp.int32)

    def x_copy(t, side, arriving):
        slot = side if arriving else 1 - side
        rows = pl.ds(0, FACES + 8 * (1 - t))
        return pltpu.make_async_remote_copy(
            src_ref=own_x.at[t, side, rows],
            dst_ref=halo_x.at[t, slot, rows],
            send_sem=sx_send.at[t, side],
            recv_sem=sx_recv.at[t, slot],
            device_id=there((1, 7)[side])[1],
            device_id_type=MESH,
        )

    def y_copy(t, index, arriving):
        d = EDGE_DIRS[index]
        slot = index if arriving else EDGE_DIRS.index(8 - d)
        rows = pl.ds(0, FR + 8 * (1 - t))
        return pltpu.make_async_remote_copy(
            src_ref=own_y.at[t, index if t == 0 else 0, rows],
            dst_ref=halo_y.at[t, slot, rows],
            send_sem=sy_send.at[t, index],
            recv_sem=sy_recv.at[t, slot],
            device_id=there(d)[1],
            device_id_type=MESH,
        )

    def send(t):
        for index in (2, 3, 4, 5, 0, 1):
            if_there(EDGE_DIRS[index], lambda: y_copy(t, index, False).start())
        for side in range(2):
            if_there((1, 7)[side], lambda: x_copy(t, side, False).start())

    lane = iota((1, 128), 1)
    lane_face = lane >> 4
    lane_pair = lane & 15

    def stacked_table(value):
        high = value.astype(BF16)
        rest = value - high.astype(F32)
        return high, jnp.concatenate([high.astype(F32), rest], axis=0).astype(BF16)

    def by_table(table, value_h, value_l):
        high, both = table
        rows = high.shape[0]
        first = dot(both, value_h)
        return first[:rows] + first[rows:] + dot(high, value_l)

    def code(entry, active):
        return jnp.where(active > 0.0, entry, -1.0)

    for load in loads[:7]:
        load.wait()
    fine, face, owner, sub, coarse, cface, level = (ints_ref[k] for k in range(7))
    shift = n_gy.bit_length() - 1
    slot = ((owner >> shift) - gx + 1) * 3 + (owner & (n_gy - 1)) - gy + 1
    count = fine.shape[1]
    hits = jnp.where(iota((16, count), 0) == slot, 1.0, 0.0)
    parts = [hits[:, k : k + EB] for k in range(0, count, EB)]
    earlier = jnp.where(iota((EB, EB), 0) < iota((EB, EB), 1), 1.0, 0.0).astype(BF16)
    within = dot(jnp.concatenate(parts, axis=0).astype(BF16), earlier)
    offset, ranks = jnp.zeros((16, 1), F32), []
    for k, part in enumerate(parts):
        ranks.append(jnp.sum(part * (within[16 * k : 16 * k + 16] + offset), axis=0, keepdims=True))
        offset = offset + jnp.sum(part, axis=1, keepdims=True)
    position = jnp.concatenate(ranks, axis=1)
    row = iota((8, count), 0)
    facts = jnp.ones((8, count), jnp.int32)
    for index, entry in enumerate((fine >> 7, fine & 127, face, coarse >> 7, coarse & 127, cface, sub)):
        facts = jnp.where(row == index, entry, facts)
    facts = facts.astype(F32)
    stacked = jnp.concatenate([facts * hits[k : k + 1] for k in range(9)], axis=0).astype(BF16)
    packed = dot_nt(stacked, one_hot(EB, position))
    for k in range(9):
        own_m[k] = packed[8 * k : 8 * k + 8]
    for side in range(2):
        d = (1, 7)[side]
        own_x[0, side, FACES : FACES + 8, :] = packed[8 * d : 8 * d + 8]
    for index, d in enumerate(EDGE_DIRS):
        own_y[0, index, FR : FR + 8, :] = packed[8 * d : 8 * d + 8]
    scale = jnp.where(level == 0, 1.0, jnp.where(level == 1, 0.5, 0.25))

    def face_product(table, value):
        high, low = split(value)
        return dot(table, high) + dot(table, low)

    def edge_values(faces):
        ends = faces[:, 0:EB]
        for a in range(1, EA):
            moved = pltpu.roll(faces[:, a * EB : (a + 1) * EB], 2 * a, 1)
            ends = jnp.where((lane == 2 * a) | (lane == 2 * a - 1), moved, ends)
        own = jnp.zeros((FR, 128), F32)
        for f in range(6):
            moved = pltpu.roll(ends[f * FR : (f + 1) * FR], 16 * f + 1, 1)
            own = jnp.where((lane_face == f) & (lane_pair < 8), moved, own)
        rows = own
        for pair, by in CORNER_SHIFT.items():
            own = jnp.where(lane_pair == pair, pltpu.roll(rows, by, 1), own)
        return own

    def edge_spread(values):
        rows = jnp.where(lane_pair < 8, values, 0.0)
        for pair, by in CORNER_SHIFT.items():
            rows = rows + jnp.where(lane_pair == pair - by, pltpu.roll(values, 128 - by, 1), 0.0)
        ends = jnp.concatenate([pltpu.roll(rows, 127 - 16 * f, 1) for f in range(6)], axis=0)
        tiles = []
        for a in range(EA):
            moved = pltpu.roll(ends, 128 - 2 * a, 1) if a else ends
            tiles.append(jnp.where((lane == 0) | (lane == EB - 1), moved, 0.0))
        return tiles

    def publish(t, faces):
        own_x[t, 0, 0:FACES, :] = faces[:, 0:EB]
        own_x[t, 1, 0:FACES, :] = faces[:, (EA - 1) * EB :]
        own = edge_values(faces)
        for index in range(6 if t == 0 else 1):
            own_y[t, index, 0:FR, :] = own
        return own

    for load in loads[7:9]:
        load.wait()
    b = b_ref[...]
    faces = face_product(pick_ref[...], b)
    own = publish(0, faces)

    pl.semaphore_wait(barrier, expected)
    send(0)

    for load in loads[9:]:
        load.wait()
    for d in range(3):
        padded = jnp.concatenate([stiff_ref[d], jnp.zeros((SP - NODES, NODES), F32)], axis=0)
        high, low = split(padded)
        stiff_s[d * SP : (d + 1) * SP, :] = high
        stiff_s[(3 + d) * SP : (4 + d) * SP, :] = low
    proj_s[...] = jnp.zeros_like(proj_s)
    proj_c[...] = jnp.zeros_like(proj_c)
    for s in range(4):
        table = proj_ref[:, s, :]
        proj_s[s * FR : s * FR + SIDE, 0:SIDE] = table
        proj_c[0:SIDE, s * FR : s * FR + SIDE] = table
    proj_t[...] = proj_s[...].T[0:FR]
    table_s = stacked_table(proj_s[0 : 4 * FR, 0:FR])
    table_c = stacked_table(proj_c[:, 0 : 4 * FR])
    table_t = stacked_table(proj_t[:, 0 : 4 * FR])

    me = own_m[4]
    self_fine = code(me[0:1] * float(EB) + me[1:2], me[7:8])
    self_coarse = code(me[3:4] * float(EB) + me[4:5], me[7:8])
    oh_self[...] = one_hot(ELEMS, jnp.concatenate([self_fine, self_coarse], axis=1))

    wide = iota((32, 512), 1)
    repeat = jnp.where(iota((32, 512), 0) == (wide >> 7) * 8 + ((wide >> 4) & 7), 1.0, 0.0).astype(BF16)
    same_pair = (iota((128, 512), 0) & 15) == (iota((128, 512), 1) & 15)
    ones = jnp.ones((16, 6 * EB), BF16)

    def edge_counts(held):
        parts_f, parts_c = [], []
        for d, facts_d in zip(EDGE_DIRS, held):
            if d in (3, 5):
                pair = facts_d[0:1] * 2.0 + (1.0 if d == 3 else 0.0)
            else:
                pair = float(CORNERS[d])
            parts_f.append(code(facts_d[2:3] * 16.0 + pair, facts_d[7:8]))
            parts_c.append(code(facts_d[6:7] * 8.0 + facts_d[5:6], facts_d[7:8]))
        fine_hot = one_hot(128, jnp.concatenate(parts_f, axis=1))
        coarse_hot = one_hot(32, jnp.concatenate(parts_c, axis=1))
        joined = dot(dot_nt(fine_hot, coarse_hot).astype(BF16), repeat)
        return jnp.where(same_pair, joined, 0.0).astype(BF16), dot_nt(ones, fine_hot)[0:1]

    n_out[...], sum_out = edge_counts([own_m[d] for d in EDGE_DIRS])

    def mortar_jump(coarses, fines, subs):
        high = coarses.astype(BF16).astype(F32)
        return by_table(table_c, by_subface(high, subs), by_subface(coarses - high, subs)) - fines

    def mortar_back(jump, subs):
        high = jump.astype(BF16).astype(F32)
        return by_table(table_t, by_subface(high, subs), by_subface(jump - high, subs))

    def local_part(field, faces):
        f_h, f_l = split(faces)
        got = dot(f_h, oh_self[...]) + dot(f_l, oh_self[...])
        jump = mortar_jump(pick_face(got[:, EB:], me[5:6]), pick_face(got[:, 0:EB], me[2:3]), me[6:7])
        back = mortar_back(jump, me[6:7])
        terms = jnp.concatenate([-PENALTY * jump, PENALTY * back], axis=1)
        s_h, s_l = spread_split(terms, jnp.concatenate([me[2:3], me[5:6]], axis=1))
        gathered = dot_nt(s_h, oh_self[...]) + dot_nt(s_l, oh_self[...])

        blocks = []
        for a in range(EA):
            here = slice(a * EB, (a + 1) * EB)
            x_low, x_high = faces[0:FR, here], faces[FR : 2 * FR, here]
            y_low, y_high = faces[2 * FR : 3 * FR, here], faces[3 * FR : 4 * FR, here]
            left = x_low if a == 0 else x_low - faces[FR : 2 * FR, (a - 1) * EB : a * EB]
            right = x_high if a == EA - 1 else x_high - faces[0:FR, (a + 1) * EB : (a + 2) * EB]
            below = jnp.where(lane == 0, 0.0, pltpu.roll(y_high, 1, 1))
            above = jnp.where(lane == EB - 1, 0.0, pltpu.roll(y_low, EB - 1, 1))
            lateral = jnp.concatenate([left, right, y_low - below, y_high - above], axis=0)
            blocks.append(jnp.concatenate([PENALTY * lateral, jnp.zeros((2 * FR, EB), F32)], axis=0))
        gathered = gathered + jnp.concatenate(blocks, axis=1)

        field_h, field_l = split(field)
        both = dot(stiff_s[...], field_h)
        rest = dot(stiff_s[0 : 3 * SP, :], field_l)
        total = field
        for d in range(3):
            here = slice(d * SP, d * SP + NODES)
            again = slice((3 + d) * SP, (3 + d) * SP + NODES)
            total = total + metric_ref[d : d + 1, :] * (both[here] + both[again] + rest[here])
        return scale * total, gathered

    def side_jumps(t, faces):
        for side in range(2):
            if_there((1, 7)[side], lambda: x_copy(t, side, True).wait_recv())
        if t == 0:
            for side in range(2):
                d = (1, 7)[side]
                both = jnp.concatenate([own_m[d], halo_x[0, side, FACES : FACES + 8, :]], axis=1)
                oh_x[side] = one_hot(EB, code(both[1:2], both[7:8]))
        fines, coarses, subs = [], [], []
        for side in range(2):
            d = (1, 7)[side]
            theirs_m = halo_x[0, side, FACES : FACES + 8, :]
            here = slice(0, EB) if side == 0 else slice((EA - 1) * EB, EA * EB)
            pair = jnp.concatenate([faces[:, here], halo_x[t, side, 0:FACES, :]], axis=0)
            high, low = split(pair)
            got = dot(high, oh_x[side]) + dot(low, oh_x[side])
            ours, theirs = got[0:FACES], got[FACES:]
            fines += [pick_face(ours[:, 0:EB], own_m[d][2:3]), pick_face(theirs[:, EB:], theirs_m[2:3])]
            coarses += [pick_face(theirs[:, 0:EB], own_m[d][5:6]), pick_face(ours[:, EB:], theirs_m[5:6])]
            subs += [own_m[d][6:7], theirs_m[6:7]]
        jump = mortar_jump(*(jnp.concatenate(parts, axis=1) for parts in (coarses, fines, subs)))
        jump = [jump[:, k * EB : (k + 1) * EB] for k in range(4)]
        energy = jnp.zeros((FR, EB), F32)
        for side in range(2):
            energy = energy - PENALTY * jump[2 * side] * fines[2 * side]
            energy = energy + PENALTY * jump[2 * side + 1] * (jump[2 * side + 1] + fines[2 * side + 1])
        energy = energy - PENALTY * faces[0:FR, 0:EB] * halo_x[t, 0, FR : 2 * FR, :]
        energy = energy - PENALTY * faces[FR : 2 * FR, (EA - 1) * EB :] * halo_x[t, 1, 0:FR, :]
        return jump, subs, jnp.sum(energy, axis=0, keepdims=True)

    def side_terms(t, jump, subs):
        back = mortar_back(jnp.concatenate([jump[1], jump[3]], axis=1), jnp.concatenate([subs[1], subs[3]], axis=1))
        result = []
        for side in range(2):
            d = (1, 7)[side]
            terms = jnp.concatenate(
                [-PENALTY * jump[2 * side], PENALTY * back[:, side * EB : (side + 1) * EB]], axis=1
            )
            theirs_m = halo_x[0, side, FACES : FACES + 8, :]
            s_h, s_l = spread_split(terms, jnp.concatenate([own_m[d][2:3], theirs_m[5:6]], axis=1))
            side_term = dot_nt(s_h, oh_x[side]) + dot_nt(s_l, oh_x[side])
            if side == 0:
                beside = [-PENALTY * halo_x[t, 0, FR : 2 * FR, :], jnp.zeros((5 * FR, EB), F32)]
            else:
                beside = [jnp.zeros((FR, EB), F32), -PENALTY * halo_x[t, 1, 0:FR, :], jnp.zeros((4 * FR, EB), F32)]
            result.append(side_term + jnp.concatenate(beside, axis=0))
        return result

    def edge_jumps(t, own, sum_in):
        for index in range(6):
            if_there(EDGE_DIRS[index], lambda: y_copy(t, index, True).wait_recv())
        if t == 0:
            n_in[...], _ = edge_counts([halo_y[0, index, FR : FR + 8, :] for index in range(6)])
            sum_in = dot(jnp.ones((16, 128), BF16), n_in[...])[0:1]
        across = jnp.zeros((FR, 128), F32)
        for index, turn in enumerate((1, -1, -3, -1, 1, 3)):
            moved = pltpu.roll(halo_y[t, index, 0:FR, :], turn % 128, 1)
            if index < 2:
                across = jnp.where((lane_pair < 8) & ((lane_pair & 1) == 1 - index), moved, across)
            else:
                across = jnp.where(lane_pair == CORNERS[EDGE_DIRS[index]], moved, across)
        pairs = jnp.concatenate([own, across], axis=1)
        pairs_h, pairs_l = split(pairs)
        images = by_table(table_s, pairs_h, pairs_l)
        image_own = jnp.concatenate([images[s * FR : (s + 1) * FR, 0:128] for s in range(4)], axis=1)
        image_far = jnp.concatenate([images[s * FR : (s + 1) * FR, 128:] for s in range(4)], axis=1)
        far_h, far_l = split(image_far)
        on_fine = own * sum_out - dot_nt(far_h, n_out[...]) - dot_nt(far_l, n_out[...])
        jumps = image_own * sum_in - dot(pairs_h[:, 128:], n_in[...]) - dot(pairs_l[:, 128:], n_in[...])
        from_low = pltpu.roll(across, 128 - 16, 1)
        from_high = pltpu.roll(across, 16, 1)
        beside = jnp.where(
            (lane_face == 2) & (lane_pair < 8) & ((lane_pair & 1) == 1),
            from_low,
            jnp.where((lane_face == 3) & (lane_pair < 8) & ((lane_pair & 1) == 0), from_high, 0.0),
        )
        direct = PENALTY * (on_fine - beside)
        energy = jnp.sum(own * direct, axis=0, keepdims=True)
        both = PENALTY * jnp.sum(image_own * jumps, axis=0, keepdims=True)
        energy = energy + sum(both[:, s * 128 : (s + 1) * 128] for s in range(4))
        return direct, jumps, energy, sum_in

    def edge_terms(direct, jumps):
        jumps = jnp.concatenate([jumps[:, s * 128 : (s + 1) * 128] for s in range(4)], axis=0)
        jumps_h, jumps_l = split(jumps)
        return edge_spread(direct + PENALTY * by_table(table_t, jumps_h, jumps_l))

    def placed(value):
        return face_product(place_ref[...], value)

    b = b_ref[...]
    total, gathered = local_part(b, faces)
    total = total + placed(gathered)
    started = face_product(pick_ref[...], total)
    jump, subs, _ = side_jumps(0, faces)
    sides = side_terms(0, jump, subs)
    direct, jumps, _, sum_in = edge_jumps(0, own, None)
    tiles = edge_terms(direct, jumps)
    tiles[0] = tiles[0] + sides[0]
    tiles[EA - 1] = tiles[EA - 1] + sides[1]
    remote = jnp.concatenate(tiles, axis=1)
    faces = started + face_product(mix_ref[...], remote)
    own = publish(1, faces)
    send(1)
    q = total + placed(remote)
    q_ref[...] = q

    total, gathered = local_part(q, faces)
    b = b_ref[...]
    q = q_ref[...]
    early = [column_sums(b, b), column_sums(b, q), column_sums(q, q)]
    energy = column_sums(q, total) + column_sums(faces, gathered)
    jump, subs, more = side_jumps(1, faces)
    energy = energy + more
    direct, jumps, more, _ = edge_jumps(1, own, sum_in)
    energy = energy + more

    lanes = jnp.zeros((1, 128), F32)
    for index, sums in enumerate(early + [energy]):
        lanes = jnp.where(lane == index, jnp.sum(sums, axis=1, keepdims=True), lanes)
    mine0[...] = lanes
    core = pltpu.make_async_remote_copy(
        src_ref=mine0,
        dst_ref=red0,
        send_sem=s0_send,
        recv_sem=s0_recv,
        device_id={"gx": gx + 1 - 2 * lax.rem(gx, 2), "gy": gy},
        device_id_type=MESH,
    )
    core.start()
    core.wait_recv()
    lanes = mine0[...] + red0[...]
    mine1[...] = lanes
    for k, offset in enumerate(chips):
        pltpu.make_async_remote_copy(
            src_ref=mine1,
            dst_ref=red1.at[k],
            send_sem=s1_send,
            recv_sem=s1_recv,
            device_id=chip(offset),
            device_id_type=MESH,
        ).start()

    sides = side_terms(1, jump, subs)
    tiles = edge_terms(direct, jumps)
    tiles[0] = tiles[0] + sides[0]
    tiles[EA - 1] = tiles[EA - 1] + sides[1]
    w_ref[...] = total + placed(gathered + jnp.concatenate(tiles, axis=1))
    for t in range(2):
        for side in range(2):
            if_there((1, 7)[side], lambda: x_copy(t, side, False).wait_send())
        for index in range(6):
            if_there(EDGE_DIRS[index], lambda: y_copy(t, index, False).wait_send())
    core.wait_send()

    pltpu.make_async_copy(red1, red1, s1_recv).wait()
    lanes = lanes + jnp.sum(red1[...], axis=0)
    bb, bq, qq, qw = (lanes[:, i : i + 1] for i in range(4))
    alpha = bb / bq
    new = bb - 2.0 * alpha * bq + alpha * alpha * qq
    grow = 1.0 + new / bb
    alpha_next = new / (grow * grow * bq - 2.0 * grow * alpha * qq + alpha * alpha * qw)
    row = iota((8, 128), 0)
    coef_ref[...] = jnp.where(row == 0, alpha + alpha_next * grow, alpha * alpha_next)
    pltpu.make_async_copy(red1, red1, s1_send).wait()


def finish(coef_ref, b_ref, q_ref, w_ref, x_hbm, r_hbm, made, out_sem):
    first, second = coef_ref[0:1, 0:1], coef_ref[1:2, 0:1]
    stores = []
    for part, (start, size) in enumerate(((0, 104), (104, NODES - 104))):
        rows = pl.ds(start, size)
        b, q, w = b_ref[rows, :], q_ref[rows, :], w_ref[rows, :]
        made[0, rows, :] = first * b - second * q
        made[1, rows, :] = b - first * q + second * w
        for k, target in enumerate((x_hbm, r_hbm)):
            store = pltpu.make_async_copy(made.at[k, rows], target.at[rows], out_sem.at[part, k])
            store.start()
            stores.append(store)
    for store in stores:
        store.wait()


def body(
    n_gx,
    n_gy,
    right_side,
    stiffness,
    metric,
    levels,
    projection,
    mortar_fine,
    mortar_face,
    mortar_owner,
    mortar_subface,
    mortar_coarse,
    mortar_cface,
):
    pick, place, mix = (jnp.asarray(table, BF16) for table in constant_tables())
    field = jax.ShapeDtypeStruct(right_side.shape, F32)
    count = mortar_fine.shape[0]
    others = n_gx // 2 * n_gy - 1
    hbm = pl.BlockSpec(memory_space=pltpu.HBM)
    vmem = pl.BlockSpec(memory_space=pltpu.VMEM)
    dma = pltpu.SemaphoreType.DMA
    line = [
        entry.reshape(1, count)
        for entry in (
            mortar_fine,
            mortar_face,
            mortar_owner,
            mortar_subface,
            mortar_coarse,
            mortar_cface,
            levels,
        )
    ]
    q, w, coef = pl.pallas_call(
        functools.partial(kernel, n_gx, n_gy),
        out_shape=(field, field, jax.ShapeDtypeStruct((8, 128), F32)),
        in_specs=[hbm] * 14,
        out_specs=(vmem, vmem, vmem),
        scratch_shapes=[
            pltpu.VMEM((NODES, ELEMS), F32),
            pltpu.VMEM((3, NODES, NODES), F32),
            pltpu.VMEM((3, ELEMS), F32),
            pltpu.VMEM((7, 1, ELEMS), jnp.int32),
            pltpu.VMEM((SIDE, 4, SIDE), F32),
            pltpu.VMEM((FACES, NODES), BF16),
            pltpu.VMEM((NODES, FACES), BF16),
            pltpu.VMEM((FACES, FACES), BF16),
            pltpu.VMEM((2, 2, FACES + 8, EB), F32),
            pltpu.VMEM((2, 6, FR + 8, 128), F32),
            pltpu.VMEM((9, 8, 128), F32),
            pltpu.VMEM((2, 2, FACES + 8, EB), F32),
            pltpu.VMEM((2, 6, FR + 8, 128), F32),
            pltpu.VMEM((6 * SP, NODES), BF16),
            pltpu.VMEM((ELEMS, 2 * EB), BF16),
            pltpu.VMEM((2, EB, 2 * EB), BF16),
            pltpu.VMEM((128, 512), BF16),
            pltpu.VMEM((128, 512), BF16),
            pltpu.VMEM((256, 128), F32),
            pltpu.VMEM((FR, 256), F32),
            pltpu.VMEM((FR, 256), F32),
            pltpu.VMEM((1, 128), F32),
            pltpu.VMEM((others, 1, 128), F32),
            pltpu.VMEM((1, 128), F32),
            pltpu.VMEM((1, 128), F32),
            dma((14,)),
            dma((2, 2)),
            dma((2, 2)),
            dma((2, 6)),
            dma((2, 6)),
            dma,
            dma,
            dma,
            dma,
        ],
        compiler_params=pltpu.CompilerParams(
            collective_id=0, has_side_effects=True, vmem_limit_bytes=40 * 1024 * 1024
        ),
    )(
        *(
            pltpu.with_memory_space_constraint(operand, pltpu.HBM)
            for operand in (right_side, stiffness, metric, *line, projection.transpose(1, 0, 2), pick, place, mix)
        )
    )
    return pl.pallas_call(
        finish,
        out_shape=(field, field),
        in_specs=[vmem] * 4,
        out_specs=(hbm, hbm),
        scratch_shapes=[pltpu.VMEM((2, NODES, ELEMS), F32), dma((2, 2))],
        compiler_params=pltpu.CompilerParams(vmem_limit_bytes=40 * 1024 * 1024),
    )(coef, right_side, q, w)


def solution(mesh):
    columns = P(None, ("gx", "gy"))
    faces = P(("gx", "gy"))
    in_specs = (columns, P(), columns, faces, P(), faces, faces, P(("gx", "gy"), None), faces, faces, faces)
    run = functools.partial(body, mesh.shape["gx"], mesh.shape["gy"])
    return jax.shard_map(run, mesh=mesh, in_specs=in_specs, out_specs=(columns, columns), check_vma=False)
```

time: 33.5 us -> 30.1 us (0.90)
  Pallas kernels: 32.7 us -> 29.3 us
    pallas_call x1, Pallas kernels: 31.6 us -> 28.2 us  [body(): pl.pallas_call(functools.partial(kernel, n_gx, n_gy), out_shape=(field, f...]
where the time goes in v3:
time: 30.1 us; the launch traced here: 30 us
  Pallas kernels  29.3 us (97%)
  between operations  0.66 us (2%)
    pallas_call x1, Pallas kernels, body(): pl.pallas_call(functools.partial(kernel, n_gx, n_gy), out_shape=(field, f...  28.2 us
    pallas_call x1, Pallas kernels, body(): pl.pallas_call(finish, out_shape=(field, field), in_specs=[vmem] * 4, out...  1.08 us

profile of v3, /device:TPU:1, one launch (start us, length us, event | category | flops | bytes accessed | tf_op | source)
XLA Modules:
  0.0 30.0 jit_solution(4888704299054486266)
XLA Ops:
  0.6 0.0 copy-start
  0.6 28.2 %shard_map.149 = (f32[216,512]{1,0:T(8,128)S(1)}, f32[216,512]{1,0:T(8,128)S(1)}, f32[8,128]{1,0:T(8,128)S(1)}) custom-call(f32[216,512]{1,0:T(8,128)} %b_ref.1, f32[3,216,216]{2,1,0:T(8,128)} %stiff_hbm.1, f32[3,512]{1,0:T(4,128)} %metric_hbm.1, s32[1,512]{1,0:T(1,128)} %bitcast.9, s32[1,512]{1,0:T(1,128)} %bitcast.10, s32[1,512]{1,0:T(1,128)} %bitcast.11, ...), custom_call_target="tpu_custom_call" | custom-call | tf_op jit(solution)/shard_map/pallas_call | solution.py:620
  28.9 0.0 copy-done
  28.9 1.1 %shard_map.150 = (f32[216,512]{1,0:T(8,128)}, f32[216,512]{1,0:T(8,128)}) custom-call(f32[8,128]{1,0:T(8,128)S(1)} %get-tuple-element.5.coef_ref, f32[216,512]{1,0:T(8,128)S(1)} %copy-done, f32[216,512]{1,0:T(8,128)S(1)} %get-tuple-element.6.q_ref, f32[216,512]{1,0:T(8,128)S(1)} %get-tuple-element.7.w_ref), custom_call_target="tpu_custom_call" | custom-call | tf_op jit(solution)/shard_map/pallas_call | solution.py:670
Async XLA Ops:
  0.6 28.2 %copy-start = (f32[216,512]{1,0:T(8,128)S(1)}, f32[216,512]{1,0:T(8,128)}, u32[]{:S(2)}) copy-start(f32[216,512]{1,0:T(8,128)} %b_ref.1) | copy-start | bytes 1327108

commit v4 on v3

--- a/solution.py
+++ b/solution.py
@@ -130,17 +130,14 @@
     proj_s,
     proj_c,
     proj_t,
-    red0,
     red1,
     mine0,
-    mine1,
     in_sem,
     sx_send,
     sx_recv,
     sy_send,
     sy_recv,
-    s0_send,
-    s0_recv,
+    ready_sem,
     s1_send,
     s1_recv,
 ):
@@ -178,10 +175,8 @@
     halo_y[...] = jnp.zeros_like(halo_y)
 
     barrier = pltpu.get_barrier_semaphore()
-    expected = jnp.int32(len(chips))
-    for offset in chips:
-        pl.semaphore_signal(barrier, inc=1, device_id=chip(offset), device_id_type=MESH)
-    for d in (0, 2, 6, 8, 1, 7):
+    expected = jnp.int32(0)
+    for d in DIRS:
         ok, where = there(d)
 
         @pl.when(ok)
@@ -214,6 +209,32 @@
             device_id=there(d)[1],
             device_id_type=MESH,
         )
+
+    rounds = [("gx", k) for k in (1, 2, 4, 8, 16) if k < n_gx] + [("gy", k) for k in (1, 2, 4, 8, 16) if k < n_gy]
+
+    def partners(k):
+        axis, by = rounds[k]
+        for step in (-by, by):
+            if axis == "gx":
+                yield (gx + step >= 0) & (gx + step < n_gx), {"gx": gx + step, "gy": gy}
+            else:
+                yield (gy + step >= 0) & (gy + step < n_gy), {"gx": gx, "gy": gy + step}
+
+    def pass_on(k):
+        for ok, where in partners(k):
+
+            @pl.when(ok)
+            def _():
+                pl.semaphore_signal(ready_sem.at[k], inc=1, device_id=where, device_id_type=MESH)
+
+    pending = list(range(len(rounds)))
+
+    def learn():
+        if pending:
+            k = pending.pop(0)
+            pl.semaphore_wait(ready_sem.at[k], sum(ok.astype(jnp.int32) for ok, _ in partners(k)))
+            if pending:
+                pass_on(k + 1)
 
     def send(t):
         for index in (2, 3, 4, 5, 0, 1):
@@ -315,6 +336,7 @@
 
     pl.semaphore_wait(barrier, expected)
     send(0)
+    pass_on(0)
 
     for load in loads[9:]:
         load.wait()
@@ -358,6 +380,7 @@
         joined = dot(dot_nt(fine_hot, coarse_hot).astype(BF16), repeat)
         return jnp.where(same_pair, joined, 0.0).astype(BF16), dot_nt(ones, fine_hot)[0:1]
 
+    learn()
     n_out[...], sum_out = edge_counts([own_m[d] for d in EDGE_DIRS])
 
     def mortar_jump(coarses, fines, subs):
@@ -490,10 +513,12 @@
     def placed(value):
         return face_product(place_ref[...], value)
 
+    learn()
     b = b_ref[...]
     total, gathered = local_part(b, faces)
     total = total + placed(gathered)
     started = face_product(pick_ref[...], total)
+    learn()
     jump, subs, _ = side_jumps(0, faces)
     sides = side_terms(0, jump, subs)
     direct, jumps, _, sum_in = edge_jumps(0, own, None)
@@ -504,14 +529,17 @@
     faces = started + face_product(mix_ref[...], remote)
     own = publish(1, faces)
     send(1)
+    learn()
     q = total + placed(remote)
     q_ref[...] = q
+    learn()
 
     total, gathered = local_part(q, faces)
     b = b_ref[...]
     q = q_ref[...]
     early = [column_sums(b, b), column_sums(b, q), column_sums(q, q)]
     energy = column_sums(q, total) + column_sums(faces, gathered)
+    learn()
     jump, subs, more = side_jumps(1, faces)
     energy = energy + more
     direct, jumps, more, _ = edge_jumps(1, own, sum_in)
@@ -521,25 +549,21 @@
     for index, sums in enumerate(early + [energy]):
         lanes = jnp.where(lane == index, jnp.sum(sums, axis=1, keepdims=True), lanes)
     mine0[...] = lanes
-    core = pltpu.make_async_remote_copy(
-        src_ref=mine0,
-        dst_ref=red0,
-        send_sem=s0_send,
-        recv_sem=s0_recv,
-        device_id={"gx": gx + 1 - 2 * lax.rem(gx, 2), "gy": gy},
-        device_id_type=MESH,
-    )
-    core.start()
-    core.wait_recv()
-    lanes = mine0[...] + red0[...]
-    mine1[...] = lanes
-    for k, offset in enumerate(chips):
+    while pending:
+        learn()
+    others = [(c, o) for o in [(0, 0, 0)] + chips for c in range(2) if c or o != (0, 0, 0)]
+    others.sort(key=lambda t: sum((v - 1) % n for v, n in zip(t[1], (size_x, size_y, size_z))))
+    for k, (flip, offset) in enumerate(others):
+        where = chip(offset)
+        if flip:
+            core = lax.rem(gx, 2)
+            where["gx"] = where["gx"] + 1 - 2 * core
         pltpu.make_async_remote_copy(
-            src_ref=mine1,
+            src_ref=mine0,
             dst_ref=red1.at[k],
             send_sem=s1_send,
             recv_sem=s1_recv,
-            device_id=chip(offset),
+            device_id=where,
             device_id_type=MESH,
         ).start()
 
@@ -553,7 +577,6 @@
             if_there((1, 7)[side], lambda: x_copy(t, side, False).wait_send())
         for index in range(6):
             if_there(EDGE_DIRS[index], lambda: y_copy(t, index, False).wait_send())
-    core.wait_send()
 
     pltpu.make_async_copy(red1, red1, s1_recv).wait()
     lanes = lanes + jnp.sum(red1[...], axis=0)
@@ -601,7 +624,7 @@
     pick, place, mix = (jnp.asarray(table, BF16) for table in constant_tables())
     field = jax.ShapeDtypeStruct(right_side.shape, F32)
     count = mortar_fine.shape[0]
-    others = n_gx // 2 * n_gy - 1
+    others = n_gx * n_gy - 1
     hbm = pl.BlockSpec(memory_space=pltpu.HBM)
     vmem = pl.BlockSpec(memory_space=pltpu.VMEM)
     dma = pltpu.SemaphoreType.DMA
@@ -644,17 +667,14 @@
             pltpu.VMEM((256, 128), F32),
             pltpu.VMEM((FR, 256), F32),
             pltpu.VMEM((FR, 256), F32),
-            pltpu.VMEM((1, 128), F32),
             pltpu.VMEM((others, 1, 128), F32),
-            pltpu.VMEM((1, 128), F32),
             pltpu.VMEM((1, 128), F32),
             dma((14,)),
             dma((2, 2)),
             dma((2, 2)),
             dma((2, 6)),
             dma((2, 6)),
-            dma,
-            dma,
+            pltpu.SemaphoreType.REGULAR((8,)),
             dma,
             dma,
         ],

time: 30.1 us -> 29 us (0.963)
  Pallas kernels: 29.3 us -> 28.2 us
    pallas_call x1, Pallas kernels: 28.2 us -> 27.1 us  [body(): pl.pallas_call(functools.partial(kernel, n_gx, n_gy), out_shape=(field, f...]
where the time goes in v4:
time: 29 us; the launch traced here: 28.9 us
  Pallas kernels  28.2 us (97%)
  between operations  0.66 us (2%)
    pallas_call x1, Pallas kernels, body(): pl.pallas_call(functools.partial(kernel, n_gx, n_gy), out_shape=(field, f...  27.1 us
    pallas_call x1, Pallas kernels, body(): pl.pallas_call(finish, out_shape=(field, field), in_specs=[vmem] * 4, out...  1.08 us

profile of v4, /device:TPU:1, one launch (start us, length us, event | category | flops | bytes accessed | tf_op | source)
XLA Modules:
  0.0 28.9 jit_solution(1837301374812045281)
XLA Ops:
  0.6 0.0 copy-start
  0.6 27.1 %shard_map.149 = (f32[216,512]{1,0:T(8,128)S(1)}, f32[216,512]{1,0:T(8,128)S(1)}, f32[8,128]{1,0:T(8,128)S(1)}) custom-call(f32[216,512]{1,0:T(8,128)} %b_ref.1, f32[3,216,216]{2,1,0:T(8,128)} %stiff_hbm.1, f32[3,512]{1,0:T(4,128)} %metric_hbm.1, s32[1,512]{1,0:T(1,128)} %bitcast.9, s32[1,512]{1,0:T(1,128)} %bitcast.10, s32[1,512]{1,0:T(1,128)} %bitcast.11, ...), custom_call_target="tpu_custom_call" | custom-call | tf_op jit(solution)/shard_map/pallas_call | solution.py:643
  27.8 0.0 copy-done
  27.8 1.1 %shard_map.150 = (f32[216,512]{1,0:T(8,128)}, f32[216,512]{1,0:T(8,128)}) custom-call(f32[8,128]{1,0:T(8,128)S(1)} %get-tuple-element.5.coef_ref, f32[216,512]{1,0:T(8,128)S(1)} %copy-done, f32[216,512]{1,0:T(8,128)S(1)} %get-tuple-element.6.q_ref, f32[216,512]{1,0:T(8,128)S(1)} %get-tuple-element.7.w_ref), custom_call_target="tpu_custom_call" | custom-call | tf_op jit(solution)/shard_map/pallas_call | solution.py:690
Async XLA Ops:
  0.6 27.2 %copy-start = (f32[216,512]{1,0:T(8,128)S(1)}, f32[216,512]{1,0:T(8,128)}, u32[]{:S(2)}) copy-start(f32[216,512]{1,0:T(8,128)} %b_ref.1) | copy-start | bytes 1327108

commit v5 on v4

--- a/solution.py
+++ b/solution.py
@@ -27,6 +27,7 @@
 EDGE_DIRS = (3, 5, 0, 2, 6, 8)
 CORNERS = {0: 8, 2: 9, 6: 10, 8: 11}
 CORNER_SHIFT = {8: 7, 9: 9, 10: 3, 11: 5}
+TURNS = (1, -1, -3, -1, 1, 3)
 
 
 def face_nodes(face):
@@ -210,15 +211,15 @@
             device_id_type=MESH,
         )
 
-    rounds = [("gx", k) for k in (1, 2, 4, 8, 16) if k < n_gx] + [("gy", k) for k in (1, 2, 4, 8, 16) if k < n_gy]
+    strides = [k for k in (1, 2, 4, 8, 16) if k < max(n_gx, n_gy)]
 
     def partners(k):
-        axis, by = rounds[k]
-        for step in (-by, by):
-            if axis == "gx":
-                yield (gx + step >= 0) & (gx + step < n_gx), {"gx": gx + step, "gy": gy}
-            else:
-                yield (gy + step >= 0) & (gy + step < n_gy), {"gx": gx, "gy": gy + step}
+        by = strides[k]
+        for dx in (-by, 0, by) if by < n_gx else (0,):
+            for dy in (-by, 0, by) if by < n_gy else (0,):
+                if dx or dy:
+                    ok = (gx + dx >= 0) & (gx + dx < n_gx) & (gy + dy >= 0) & (gy + dy < n_gy)
+                    yield ok, {"gx": gx + dx, "gy": gy + dy}
 
     def pass_on(k):
         for ok, where in partners(k):
@@ -227,7 +228,7 @@
             def _():
                 pl.semaphore_signal(ready_sem.at[k], inc=1, device_id=where, device_id_type=MESH)
 
-    pending = list(range(len(rounds)))
+    pending = list(range(len(strides)))
 
     def learn():
         if pending:
@@ -260,7 +261,7 @@
     def code(entry, active):
         return jnp.where(active > 0.0, entry, -1.0)
 
-    for load in loads[:7]:
+    for load in loads[:9]:
         load.wait()
     fine, face, owner, sub, coarse, cface, level = (ints_ref[k] for k in range(7))
     shift = n_gy.bit_length() - 1
@@ -328,8 +329,6 @@
             own_y[t, index, 0:FR, :] = own
         return own
 
-    for load in loads[7:9]:
-        load.wait()
     b = b_ref[...]
     faces = face_product(pick_ref[...], b)
     own = publish(0, faces)
@@ -380,7 +379,6 @@
         joined = dot(dot_nt(fine_hot, coarse_hot).astype(BF16), repeat)
         return jnp.where(same_pair, joined, 0.0).astype(BF16), dot_nt(ones, fine_hot)[0:1]
 
-    learn()
     n_out[...], sum_out = edge_counts([own_m[d] for d in EDGE_DIRS])
 
     def mortar_jump(coarses, fines, subs):
@@ -423,20 +421,17 @@
             total = total + metric_ref[d : d + 1, :] * (both[here] + both[again] + rest[here])
         return scale * total, gathered
 
-    def side_jumps(t, faces):
-        for side in range(2):
-            if_there((1, 7)[side], lambda: x_copy(t, side, True).wait_recv())
-        if t == 0:
-            for side in range(2):
-                d = (1, 7)[side]
-                both = jnp.concatenate([own_m[d], halo_x[0, side, FACES : FACES + 8, :]], axis=1)
-                oh_x[side] = one_hot(EB, code(both[1:2], both[7:8]))
+    def side_jumps(faces):
+        for side in range(2):
+            d = (1, 7)[side]
+            both = jnp.concatenate([own_m[d], halo_x[0, side, FACES : FACES + 8, :]], axis=1)
+            oh_x[side] = one_hot(EB, code(both[1:2], both[7:8]))
         fines, coarses, subs = [], [], []
         for side in range(2):
             d = (1, 7)[side]
             theirs_m = halo_x[0, side, FACES : FACES + 8, :]
             here = slice(0, EB) if side == 0 else slice((EA - 1) * EB, EA * EB)
-            pair = jnp.concatenate([faces[:, here], halo_x[t, side, 0:FACES, :]], axis=0)
+            pair = jnp.concatenate([faces[:, here], halo_x[0, side, 0:FACES, :]], axis=0)
             high, low = split(pair)
             got = dot(high, oh_x[side]) + dot(low, oh_x[side])
             ours, theirs = got[0:FACES], got[FACES:]
@@ -445,13 +440,51 @@
             subs += [own_m[d][6:7], theirs_m[6:7]]
         jump = mortar_jump(*(jnp.concatenate(parts, axis=1) for parts in (coarses, fines, subs)))
         jump = [jump[:, k * EB : (k + 1) * EB] for k in range(4)]
-        energy = jnp.zeros((FR, EB), F32)
-        for side in range(2):
-            energy = energy - PENALTY * jump[2 * side] * fines[2 * side]
-            energy = energy + PENALTY * jump[2 * side + 1] * (jump[2 * side + 1] + fines[2 * side + 1])
-        energy = energy - PENALTY * faces[0:FR, 0:EB] * halo_x[t, 0, FR : 2 * FR, :]
-        energy = energy - PENALTY * faces[FR : 2 * FR, (EA - 1) * EB :] * halo_x[t, 1, 0:FR, :]
-        return jump, subs, jnp.sum(energy, axis=0, keepdims=True)
+        return jump, subs
+
+    def side_adjoint(faces):
+        fines, coarses, subs = [], [], []
+        for side in range(2):
+            d = (1, 7)[side]
+            theirs_m = halo_x[0, side, FACES : FACES + 8, :]
+            high, low = split(faces[:, 0:EB] if side == 0 else faces[:, (EA - 1) * EB :])
+            got = dot(high, oh_x[side]) + dot(low, oh_x[side])
+            fines.append(pick_face(got[:, 0:EB], own_m[d][2:3]))
+            coarses.append(pick_face(got[:, EB:], theirs_m[5:6]))
+            subs += [own_m[d][6:7], theirs_m[6:7]]
+        fines = jnp.concatenate(fines, axis=1)
+        images = mortar_jump(jnp.concatenate(coarses, axis=1), 0.0, jnp.concatenate([subs[1], subs[3]], axis=1))
+        backs = mortar_back(fines, jnp.concatenate([subs[0], subs[2]], axis=1))
+        against = []
+        for side in range(2):
+            d = (1, 7)[side]
+            here = slice(side * EB, (side + 1) * EB)
+            theirs_m = halo_x[0, side, FACES : FACES + 8, :]
+            s_h, s_l = spread_split(
+                jnp.concatenate([backs[:, here], images[:, here]], axis=1),
+                jnp.concatenate([own_m[d][5:6], theirs_m[2:3]], axis=1),
+            )
+            against.append(dot_nt(s_h, oh_x[side]) + dot_nt(s_l, oh_x[side]))
+        low_face, high_face = faces[0:FR, 0:EB], faces[FR : 2 * FR, (EA - 1) * EB :]
+        against[0] = against[0] + jnp.concatenate([jnp.zeros((FR, EB), F32), low_face, jnp.zeros((4 * FR, EB), F32)], axis=0)
+        against[1] = against[1] + jnp.concatenate([high_face, jnp.zeros((5 * FR, EB), F32)], axis=0)
+        known = jnp.sum(fines * fines + images * images, axis=0, keepdims=True)
+        return fines, images, subs, against, known[:, 0:EB] + known[:, EB:]
+
+    def side_jumps_after(fines, images, subs):
+        far_fines, far_coarses = [], []
+        for side in range(2):
+            d = (1, 7)[side]
+            theirs_m = halo_x[0, side, FACES : FACES + 8, :]
+            high, low = split(halo_x[1, side, 0:FACES, :])
+            got = dot(high, oh_x[side]) + dot(low, oh_x[side])
+            far_coarses.append(pick_face(got[:, 0:EB], own_m[d][5:6]))
+            far_fines.append(pick_face(got[:, EB:], theirs_m[2:3]))
+        out = mortar_jump(
+            jnp.concatenate(far_coarses, axis=1), fines, jnp.concatenate([subs[0], subs[2]], axis=1)
+        )
+        into = images - jnp.concatenate(far_fines, axis=1)
+        return [out[:, 0:EB], into[:, 0:EB], out[:, EB:], into[:, EB:]]
 
     def side_terms(t, jump, subs):
         back = mortar_back(jnp.concatenate([jump[1], jump[3]], axis=1), jnp.concatenate([subs[1], subs[3]], axis=1))
@@ -471,19 +504,26 @@
             result.append(side_term + jnp.concatenate(beside, axis=0))
         return result
 
-    def edge_jumps(t, own, sum_in):
+    low_face = (lane_face == 2) & (lane_pair < 8) & ((lane_pair & 1) == 1)
+    high_face = (lane_face == 3) & (lane_pair < 8) & ((lane_pair & 1) == 0)
+
+    def pair_mask(index):
+        if index < 2:
+            return (lane_pair < 8) & ((lane_pair & 1) == 1 - index)
+        return lane_pair == CORNERS[EDGE_DIRS[index]]
+
+    def edges_arrive(t):
         for index in range(6):
             if_there(EDGE_DIRS[index], lambda: y_copy(t, index, True).wait_recv())
-        if t == 0:
-            n_in[...], _ = edge_counts([halo_y[0, index, FR : FR + 8, :] for index in range(6)])
-            sum_in = dot(jnp.ones((16, 128), BF16), n_in[...])[0:1]
+
+    def sides_arrive(t):
+        for side in range(2):
+            if_there((1, 7)[side], lambda: x_copy(t, side, True).wait_recv())
+
+    def edge_jumps(t, own, sum_in):
         across = jnp.zeros((FR, 128), F32)
-        for index, turn in enumerate((1, -1, -3, -1, 1, 3)):
-            moved = pltpu.roll(halo_y[t, index, 0:FR, :], turn % 128, 1)
-            if index < 2:
-                across = jnp.where((lane_pair < 8) & ((lane_pair & 1) == 1 - index), moved, across)
-            else:
-                across = jnp.where(lane_pair == CORNERS[EDGE_DIRS[index]], moved, across)
+        for index, turn in enumerate(TURNS):
+            across = jnp.where(pair_mask(index), pltpu.roll(halo_y[t, index, 0:FR, :], turn % 128, 1), across)
         pairs = jnp.concatenate([own, across], axis=1)
         pairs_h, pairs_l = split(pairs)
         images = by_table(table_s, pairs_h, pairs_l)
@@ -494,16 +534,25 @@
         jumps = image_own * sum_in - dot(pairs_h[:, 128:], n_in[...]) - dot(pairs_l[:, 128:], n_in[...])
         from_low = pltpu.roll(across, 128 - 16, 1)
         from_high = pltpu.roll(across, 16, 1)
-        beside = jnp.where(
-            (lane_face == 2) & (lane_pair < 8) & ((lane_pair & 1) == 1),
-            from_low,
-            jnp.where((lane_face == 3) & (lane_pair < 8) & ((lane_pair & 1) == 0), from_high, 0.0),
-        )
-        direct = PENALTY * (on_fine - beside)
-        energy = jnp.sum(own * direct, axis=0, keepdims=True)
-        both = PENALTY * jnp.sum(image_own * jumps, axis=0, keepdims=True)
-        energy = energy + sum(both[:, s * 128 : (s + 1) * 128] for s in range(4))
-        return direct, jumps, energy, sum_in
+        beside = jnp.where(low_face, from_low, jnp.where(high_face, from_high, 0.0))
+        return PENALTY * (on_fine - beside), jumps
+
+    def edge_adjoint(own, sum_in):
+        own_h, own_l = split(own)
+        images = by_table(table_s, own_h, own_l)
+        images = jnp.concatenate([images[s * FR : (s + 1) * FR] for s in range(4)], axis=1)
+        images_h, images_l = split(images)
+        joined = dot(own_h, n_out[...]) + dot(own_l, n_out[...])
+        joined_h, joined_l = split(jnp.concatenate([joined[:, s * 128 : (s + 1) * 128] for s in range(4)], axis=0))
+        meets = by_table(table_t, joined_h, joined_l) + dot_nt(images_h, n_in[...]) + dot_nt(images_l, n_in[...])
+        meets = meets + pltpu.roll(jnp.where(low_face, own, 0.0), 16, 1)
+        meets = meets + pltpu.roll(jnp.where(high_face, own, 0.0), 128 - 16, 1)
+        against = []
+        for index, turn in enumerate(TURNS):
+            against.append(pltpu.roll(jnp.where(pair_mask(index), meets, 0.0), -turn % 128, 1))
+        known = jnp.sum(own * own * sum_out, axis=0, keepdims=True)
+        both = jnp.sum(images * images * sum_in, axis=0, keepdims=True)
+        return against, known + sum(both[:, s * 128 : (s + 1) * 128] for s in range(4))
 
     def edge_terms(direct, jumps):
         jumps = jnp.concatenate([jumps[:, s * 128 : (s + 1) * 128] for s in range(4)], axis=0)
@@ -519,9 +568,13 @@
     total = total + placed(gathered)
     started = face_product(pick_ref[...], total)
     learn()
-    jump, subs, _ = side_jumps(0, faces)
+    sides_arrive(0)
+    jump, subs = side_jumps(faces)
     sides = side_terms(0, jump, subs)
-    direct, jumps, _, sum_in = edge_jumps(0, own, None)
+    edges_arrive(0)
+    n_in[...], _ = edge_counts([halo_y[0, index, FR : FR + 8, :] for index in range(6)])
+    sum_in = dot(jnp.ones((16, 128), BF16), n_in[...])[0:1]
+    direct, jumps = edge_jumps(0, own, sum_in)
     tiles = edge_terms(direct, jumps)
     tiles[0] = tiles[0] + sides[0]
     tiles[EA - 1] = tiles[EA - 1] + sides[1]
@@ -532,18 +585,24 @@
     learn()
     q = total + placed(remote)
     q_ref[...] = q
-    learn()
 
     total, gathered = local_part(q, faces)
     b = b_ref[...]
     q = q_ref[...]
     early = [column_sums(b, b), column_sums(b, q), column_sums(q, q)]
     energy = column_sums(q, total) + column_sums(faces, gathered)
-    learn()
-    jump, subs, more = side_jumps(1, faces)
-    energy = energy + more
-    direct, jumps, more, _ = edge_jumps(1, own, sum_in)
-    energy = energy + more
+    fines, images, subs, side_against, known = side_adjoint(faces)
+    energy = energy + PENALTY * known
+    edge_against, known = edge_adjoint(own, sum_in)
+    energy = energy + PENALTY * known
+    sides_arrive(1)
+    met = jnp.zeros((1, 128), F32)
+    for side in range(2):
+        met = met + jnp.sum(halo_x[1, side, 0:FACES, :] * side_against[side], axis=0, keepdims=True)
+    energy = energy - PENALTY * met
+    edges_arrive(1)
+    met = sum(halo_y[1, index, 0:FR, :] * edge_against[index] for index in range(6))
+    energy = energy - PENALTY * jnp.sum(met, axis=0, keepdims=True)
 
     lanes = jnp.zeros((1, 128), F32)
     for index, sums in enumerate(early + [energy]):
@@ -567,8 +626,8 @@
             device_id_type=MESH,
         ).start()
 
-    sides = side_terms(1, jump, subs)
-    tiles = edge_terms(direct, jumps)
+    sides = side_terms(1, side_jumps_after(fines, images, subs), subs)
+    tiles = edge_terms(*edge_jumps(1, own, sum_in))
     tiles[0] = tiles[0] + sides[0]
     tiles[EA - 1] = tiles[EA - 1] + sides[1]
     w_ref[...] = total + placed(gathered + jnp.concatenate(tiles, axis=1))

time: 29 us -> 28.2 us (0.972)
  Pallas kernels: 28.2 us -> 27.4 us
    pallas_call x1, Pallas kernels: 27.1 us -> 26.3 us  [body(): pl.pallas_call(functools.partial(kernel, n_gx, n_gy), out_shape=(field, f...]
where the time goes in v5:
time: 28.2 us; the launch traced here: 28 us
  Pallas kernels  27.4 us (97%)
  between operations  0.66 us (2%)
    pallas_call x1, Pallas kernels, body(): pl.pallas_call(functools.partial(kernel, n_gx, n_gy), out_shape=(field, f...  26.3 us
    pallas_call x1, Pallas kernels, body(): pl.pallas_call(finish, out_shape=(field, field), in_specs=[vmem] * 4, out...  1.08 us

profile of v5, /device:TPU:1, one launch (start us, length us, event | category | flops | bytes accessed | tf_op | source)
XLA Modules:
  0.0 28.0 jit_solution(12382286683465108988)
XLA Ops:
  0.6 0.0 copy-start
  0.6 26.3 %shard_map.149 = (f32[216,512]{1,0:T(8,128)S(1)}, f32[216,512]{1,0:T(8,128)S(1)}, f32[8,128]{1,0:T(8,128)S(1)}) custom-call(f32[216,512]{1,0:T(8,128)} %b_ref.1, f32[3,216,216]{2,1,0:T(8,128)} %stiff_hbm.1, f32[3,512]{1,0:T(4,128)} %metric_hbm.1, s32[1,512]{1,0:T(1,128)} %bitcast.9, s32[1,512]{1,0:T(1,128)} %bitcast.10, s32[1,512]{1,0:T(1,128)} %bitcast.11, ...), custom_call_target="tpu_custom_call" | custom-call | tf_op jit(solution)/shard_map/pallas_call | solution.py:702
  27.0 0.0 copy-done
  27.0 1.1 %shard_map.150 = (f32[216,512]{1,0:T(8,128)}, f32[216,512]{1,0:T(8,128)}) custom-call(f32[8,128]{1,0:T(8,128)S(1)} %get-tuple-element.5.coef_ref, f32[216,512]{1,0:T(8,128)S(1)} %copy-done, f32[216,512]{1,0:T(8,128)S(1)} %get-tuple-element.6.q_ref, f32[216,512]{1,0:T(8,128)S(1)} %get-tuple-element.7.w_ref), custom_call_target="tpu_custom_call" | custom-call | tf_op jit(solution)/shard_map/pallas_call | solution.py:749
Async XLA Ops:
  0.6 26.3 %copy-start = (f32[216,512]{1,0:T(8,128)S(1)}, f32[216,512]{1,0:T(8,128)}, u32[]{:S(2)}) copy-start(f32[216,512]{1,0:T(8,128)} %b_ref.1) | copy-start | bytes 1327108

commit v6 on v5

--- a/solution.py
+++ b/solution.py
@@ -25,9 +25,10 @@
 
 DIRS = {d: (d // 3 - 1, d % 3 - 1) for d in range(9) if d != 4}
 EDGE_DIRS = (3, 5, 0, 2, 6, 8)
-CORNERS = {0: 8, 2: 9, 6: 10, 8: 11}
-CORNER_SHIFT = {8: 7, 9: 9, 10: 3, 11: 5}
-TURNS = (1, -1, -3, -1, 1, 3)
+CORNERS = {0: 8, 2: 10, 6: 12, 8: 14}
+CORNER_SHIFT = {8: 7, 10: 10, 12: 5, 14: 8}
+PACK = {(f, g): 8 * ((5 * f + g) // 2) + (5 * f + g) % 2 for f in range(6) for g in range(FR // 8)}
+CORNER_ROWS = (EA - 1, EA - 1, 0, 0)
 
 
 def face_nodes(face):
@@ -201,9 +202,9 @@
     def y_copy(t, index, arriving):
         d = EDGE_DIRS[index]
         slot = index if arriving else EDGE_DIRS.index(8 - d)
-        rows = pl.ds(0, FR + 8 * (1 - t))
+        rows = pl.ds(0, 8 + 8 * (1 - t))
         return pltpu.make_async_remote_copy(
-            src_ref=own_y.at[t, index if t == 0 else 0, rows],
+            src_ref=own_y.at[t, index, rows],
             dst_ref=halo_y.at[t, slot, rows],
             send_sem=sy_send.at[t, index],
             recv_sem=sy_recv.at[t, slot],
@@ -289,18 +290,21 @@
         d = (1, 7)[side]
         own_x[0, side, FACES : FACES + 8, :] = packed[8 * d : 8 * d + 8]
     for index, d in enumerate(EDGE_DIRS):
-        own_y[0, index, FR : FR + 8, :] = packed[8 * d : 8 * d + 8]
+        own_y[0, index, 8:16, :] = packed[8 * d : 8 * d + 8]
     scale = jnp.where(level == 0, 1.0, jnp.where(level == 1, 0.5, 0.25))
 
     def face_product(table, value):
         high, low = split(value)
         return dot(table, high) + dot(table, low)
 
-    def edge_values(faces):
+    def edge_ends(faces):
         ends = faces[:, 0:EB]
         for a in range(1, EA):
             moved = pltpu.roll(faces[:, a * EB : (a + 1) * EB], 2 * a, 1)
             ends = jnp.where((lane == 2 * a) | (lane == 2 * a - 1), moved, ends)
+        return ends
+
+    def edge_values(ends):
         own = jnp.zeros((FR, 128), F32)
         for f in range(6):
             moved = pltpu.roll(ends[f * FR : (f + 1) * FR], 16 * f + 1, 1)
@@ -309,6 +313,36 @@
         for pair, by in CORNER_SHIFT.items():
             own = jnp.where(lane_pair == pair, pltpu.roll(rows, by, 1), own)
         return own
+
+    def lanes_of(start):
+        return (lane >= start) & (lane < start + 8) & ((lane & 1) == start % 2)
+
+    def pack(part, turn):
+        result = jnp.zeros((8, 128), F32)
+        for (f, g), start in PACK.items():
+            result = jnp.where(lanes_of(start), pltpu.roll(part(f, g), (start + turn(f)) % 128, 1), result)
+        return result
+
+    def pack_pairs(values, first):
+        return pack(lambda f, g: values[8 * g : 8 * g + 8], lambda f: -16 * f - first)
+
+    def corner_lanes(c):
+        return ((lane & 7) >> 1) == c
+
+    def edge_across(t):
+        corners = jnp.zeros((8, 128), F32)
+        for c, a in enumerate(CORNER_ROWS):
+            moved = pltpu.roll(halo_y[t, 2 + c, 0:8, :], 2 * (c - a) % 128, 1)
+            corners = jnp.where(corner_lanes(c), moved, corners)
+        groups = []
+        for g in range(FR // 8):
+            group = jnp.zeros((8, 128), F32)
+            for packed_rows, first in ((halo_y[t, 0, 0:8, :], 1), (halo_y[t, 1, 0:8, :], 0), (corners, 8)):
+                for f in range(6):
+                    moved = pltpu.roll(packed_rows, (16 * f + first - PACK[f, g]) % 128, 1)
+                    group = jnp.where(lanes_of(16 * f + first), moved, group)
+            groups.append(group)
+        return jnp.concatenate(groups, axis=0)
 
     def edge_spread(values):
         rows = jnp.where(lane_pair < 8, values, 0.0)
@@ -324,18 +358,24 @@
     def publish(t, faces):
         own_x[t, 0, 0:FACES, :] = faces[:, 0:EB]
         own_x[t, 1, 0:FACES, :] = faces[:, (EA - 1) * EB :]
-        own = edge_values(faces)
-        for index in range(6 if t == 0 else 1):
-            own_y[t, index, 0:FR, :] = own
-        return own
+        ends = edge_ends(faces)
+
+        def rows(f, g):
+            return ends[f * FR + 8 * g : f * FR + 8 * g + 8]
+
+        toward = (pack(rows, lambda f: 0), pack(rows, lambda f: 1))
+        for index, d in enumerate(EDGE_DIRS):
+            own_y[t, index, 0:8, :] = toward[0 if DIRS[d][1] < 0 else 1]
+        return ends
 
     b = b_ref[...]
     faces = face_product(pick_ref[...], b)
-    own = publish(0, faces)
+    ends = publish(0, faces)
 
     pl.semaphore_wait(barrier, expected)
     send(0)
     pass_on(0)
+    own = edge_values(ends)
 
     for load in loads[9:]:
         load.wait()
@@ -507,11 +547,6 @@
     low_face = (lane_face == 2) & (lane_pair < 8) & ((lane_pair & 1) == 1)
     high_face = (lane_face == 3) & (lane_pair < 8) & ((lane_pair & 1) == 0)
 
-    def pair_mask(index):
-        if index < 2:
-            return (lane_pair < 8) & ((lane_pair & 1) == 1 - index)
-        return lane_pair == CORNERS[EDGE_DIRS[index]]
-
     def edges_arrive(t):
         for index in range(6):
             if_there(EDGE_DIRS[index], lambda: y_copy(t, index, True).wait_recv())
@@ -521,9 +556,7 @@
             if_there((1, 7)[side], lambda: x_copy(t, side, True).wait_recv())
 
     def edge_jumps(t, own, sum_in):
-        across = jnp.zeros((FR, 128), F32)
-        for index, turn in enumerate(TURNS):
-            across = jnp.where(pair_mask(index), pltpu.roll(halo_y[t, index, 0:FR, :], turn % 128, 1), across)
+        across = edge_across(t)
         pairs = jnp.concatenate([own, across], axis=1)
         pairs_h, pairs_l = split(pairs)
         images = by_table(table_s, pairs_h, pairs_l)
@@ -547,9 +580,10 @@
         meets = by_table(table_t, joined_h, joined_l) + dot_nt(images_h, n_in[...]) + dot_nt(images_l, n_in[...])
         meets = meets + pltpu.roll(jnp.where(low_face, own, 0.0), 16, 1)
         meets = meets + pltpu.roll(jnp.where(high_face, own, 0.0), 128 - 16, 1)
-        against = []
-        for index, turn in enumerate(TURNS):
-            against.append(pltpu.roll(jnp.where(pair_mask(index), meets, 0.0), -turn % 128, 1))
+        against = [pack_pairs(meets, 1), pack_pairs(meets, 0)]
+        corners = pack_pairs(meets, 8)
+        for c, a in enumerate(CORNER_ROWS):
+            against.append(pltpu.roll(jnp.where(corner_lanes(c), corners, 0.0), 2 * (a - c) % 128, 1))
         known = jnp.sum(own * own * sum_out, axis=0, keepdims=True)
         both = jnp.sum(images * images * sum_in, axis=0, keepdims=True)
         return against, known + sum(both[:, s * 128 : (s + 1) * 128] for s in range(4))
@@ -572,7 +606,7 @@
     jump, subs = side_jumps(faces)
     sides = side_terms(0, jump, subs)
     edges_arrive(0)
-    n_in[...], _ = edge_counts([halo_y[0, index, FR : FR + 8, :] for index in range(6)])
+    n_in[...], _ = edge_counts([halo_y[0, index, 8:16, :] for index in range(6)])
     sum_in = dot(jnp.ones((16, 128), BF16), n_in[...])[0:1]
     direct, jumps = edge_jumps(0, own, sum_in)
     tiles = edge_terms(direct, jumps)
@@ -580,9 +614,10 @@
     tiles[EA - 1] = tiles[EA - 1] + sides[1]
     remote = jnp.concatenate(tiles, axis=1)
     faces = started + face_product(mix_ref[...], remote)
-    own = publish(1, faces)
+    ends = publish(1, faces)
     send(1)
     learn()
+    own = edge_values(ends)
     q = total + placed(remote)
     q_ref[...] = q
 
@@ -601,7 +636,7 @@
         met = met + jnp.sum(halo_x[1, side, 0:FACES, :] * side_against[side], axis=0, keepdims=True)
     energy = energy - PENALTY * met
     edges_arrive(1)
-    met = sum(halo_y[1, index, 0:FR, :] * edge_against[index] for index in range(6))
+    met = sum(halo_y[1, index, 0:8, :] * edge_against[index] for index in range(6))
     energy = energy - PENALTY * jnp.sum(met, axis=0, keepdims=True)
 
     lanes = jnp.zeros((1, 128), F32)
@@ -714,10 +749,10 @@
             pltpu.VMEM((NODES, FACES), BF16),
             pltpu.VMEM((FACES, FACES), BF16),
             pltpu.VMEM((2, 2, FACES + 8, EB), F32),
-            pltpu.VMEM((2, 6, FR + 8, 128), F32),
+            pltpu.VMEM((2, 6, 16, 128), F32),
             pltpu.VMEM((9, 8, 128), F32),
             pltpu.VMEM((2, 2, FACES + 8, EB), F32),
-            pltpu.VMEM((2, 6, FR + 8, 128), F32),
+            pltpu.VMEM((2, 6, 16, 128), F32),
             pltpu.VMEM((6 * SP, NODES), BF16),
             pltpu.VMEM((ELEMS, 2 * EB), BF16),
             pltpu.VMEM((2, EB, 2 * EB), BF16),

time: 28.2 us -> 27.6 us (0.979)
  Pallas kernels: 27.4 us -> 26.9 us
    pallas_call x1, Pallas kernels: 26.3 us -> 25.8 us  [body(): pl.pallas_call(functools.partial(kernel, n_gx, n_gy), out_shape=(field, f...]
where the time goes in v6:
time: 27.6 us; the launch traced here: 27.5 us
  Pallas kernels  26.9 us (97%)
  between operations  0.66 us (2%)
    pallas_call x1, Pallas kernels, body(): pl.pallas_call(functools.partial(kernel, n_gx, n_gy), out_shape=(field, f...  25.8 us
    pallas_call x1, Pallas kernels, body(): pl.pallas_call(finish, out_shape=(field, field), in_specs=[vmem] * 4, out...  1.08 us

profile of v6, /device:TPU:1, one launch (start us, length us, event | category | flops | bytes accessed | tf_op | source)
XLA Modules:
  0.0 27.5 jit_solution(16063503311229546121)
XLA Ops:
  0.6 0.0 copy-start
  0.6 25.8 %shard_map.149 = (f32[216,512]{1,0:T(8,128)S(1)}, f32[216,512]{1,0:T(8,128)S(1)}, f32[8,128]{1,0:T(8,128)S(1)}) custom-call(f32[216,512]{1,0:T(8,128)} %b_ref.1, f32[3,216,216]{2,1,0:T(8,128)} %stiff_hbm.1, f32[3,512]{1,0:T(4,128)} %metric_hbm.1, s32[1,512]{1,0:T(1,128)} %bitcast.9, s32[1,512]{1,0:T(1,128)} %bitcast.10, s32[1,512]{1,0:T(1,128)} %bitcast.11, ...), custom_call_target="tpu_custom_call" | custom-call | tf_op jit(solution)/shard_map/pallas_call | solution.py:737
  26.4 0.0 copy-done
  26.4 1.1 %shard_map.150 = (f32[216,512]{1,0:T(8,128)}, f32[216,512]{1,0:T(8,128)}) custom-call(f32[8,128]{1,0:T(8,128)S(1)} %get-tuple-element.5.coef_ref, f32[216,512]{1,0:T(8,128)S(1)} %copy-done, f32[216,512]{1,0:T(8,128)S(1)} %get-tuple-element.6.q_ref, f32[216,512]{1,0:T(8,128)S(1)} %get-tuple-element.7.w_ref), custom_call_target="tpu_custom_call" | custom-call | tf_op jit(solution)/shard_map/pallas_call | solution.py:784
Async XLA Ops:
  0.6 25.8 %copy-start = (f32[216,512]{1,0:T(8,128)S(1)}, f32[216,512]{1,0:T(8,128)}, u32[]{:S(2)}) copy-start(f32[216,512]{1,0:T(8,128)} %b_ref.1) | copy-start | bytes 1327108

commit v7 on v6

--- a/solution.py
+++ b/solution.py
@@ -596,16 +596,15 @@
     def placed(value):
         return face_product(place_ref[...], value)
 
-    learn()
     b = b_ref[...]
     total, gathered = local_part(b, faces)
+    learn()
     total = total + placed(gathered)
     started = face_product(pick_ref[...], total)
-    learn()
     sides_arrive(0)
+    edges_arrive(0)
     jump, subs = side_jumps(faces)
     sides = side_terms(0, jump, subs)
-    edges_arrive(0)
     n_in[...], _ = edge_counts([halo_y[0, index, 8:16, :] for index in range(6)])
     sum_in = dot(jnp.ones((16, 128), BF16), n_in[...])[0:1]
     direct, jumps = edge_jumps(0, own, sum_in)
@@ -624,6 +623,7 @@
     total, gathered = local_part(q, faces)
     b = b_ref[...]
     q = q_ref[...]
+    learn()
     early = [column_sums(b, b), column_sums(b, q), column_sums(q, q)]
     energy = column_sums(q, total) + column_sums(faces, gathered)
     fines, images, subs, side_against, known = side_adjoint(faces)

time: 27.6 us -> 26.7 us (0.967)
  Pallas kernels: 26.9 us -> 25.9 us
    pallas_call x1, Pallas kernels: 25.8 us -> 24.9 us  [body(): pl.pallas_call(functools.partial(kernel, n_gx, n_gy), out_shape=(field, f...]
where the time goes in v7:
time: 26.7 us; the launch traced here: 26.6 us
  Pallas kernels  25.9 us (97%)
  between operations  0.66 us (2%)
    pallas_call x1, Pallas kernels, body(): pl.pallas_call(functools.partial(kernel, n_gx, n_gy), out_shape=(field, f...  24.9 us
    pallas_call x1, Pallas kernels, body(): pl.pallas_call(finish, out_shape=(field, field), in_specs=[vmem] * 4, out...  1.08 us

profile of v7, /device:TPU:1, one launch (start us, length us, event | category | flops | bytes accessed | tf_op | source)
XLA Modules:
  0.0 26.6 jit_solution(7723742579301868682)
XLA Ops:
  0.6 0.0 copy-start
  0.6 24.9 %shard_map.149 = (f32[216,512]{1,0:T(8,128)S(1)}, f32[216,512]{1,0:T(8,128)S(1)}, f32[8,128]{1,0:T(8,128)S(1)}) custom-call(f32[216,512]{1,0:T(8,128)} %b_ref.1, f32[3,216,216]{2,1,0:T(8,128)} %stiff_hbm.1, f32[3,512]{1,0:T(4,128)} %metric_hbm.1, s32[1,512]{1,0:T(1,128)} %bitcast.9, s32[1,512]{1,0:T(1,128)} %bitcast.10, s32[1,512]{1,0:T(1,128)} %bitcast.11, ...), custom_call_target="tpu_custom_call" | custom-call | tf_op jit(solution)/shard_map/pallas_call | solution.py:737
  25.5 0.0 copy-done
  25.5 1.1 %shard_map.150 = (f32[216,512]{1,0:T(8,128)}, f32[216,512]{1,0:T(8,128)}) custom-call(f32[8,128]{1,0:T(8,128)S(1)} %get-tuple-element.5.coef_ref, f32[216,512]{1,0:T(8,128)S(1)} %copy-done, f32[216,512]{1,0:T(8,128)S(1)} %get-tuple-element.6.q_ref, f32[216,512]{1,0:T(8,128)S(1)} %get-tuple-element.7.w_ref), custom_call_target="tpu_custom_call" | custom-call | tf_op jit(solution)/shard_map/pallas_call | solution.py:784
Async XLA Ops:
  0.6 24.9 %copy-start = (f32[216,512]{1,0:T(8,128)S(1)}, f32[216,512]{1,0:T(8,128)}, u32[]{:S(2)}) copy-start(f32[216,512]{1,0:T(8,128)} %b_ref.1) | copy-start | bytes 1327108

commit v8 on v7

--- a/solution.py
+++ b/solution.py
@@ -654,7 +654,7 @@
             where["gx"] = where["gx"] + 1 - 2 * core
         pltpu.make_async_remote_copy(
             src_ref=mine0,
-            dst_ref=red1.at[k],
+            dst_ref=red1.at[pl.ds(k, 1)],
             send_sem=s1_send,
             recv_sem=s1_recv,
             device_id=where,
@@ -673,7 +673,7 @@
             if_there(EDGE_DIRS[index], lambda: y_copy(t, index, False).wait_send())
 
     pltpu.make_async_copy(red1, red1, s1_recv).wait()
-    lanes = lanes + jnp.sum(red1[...], axis=0)
+    lanes = lanes + jnp.sum(red1[...], axis=0, keepdims=True)
     bb, bq, qq, qw = (lanes[:, i : i + 1] for i in range(4))
     alpha = bb / bq
     new = bb - 2.0 * alpha * bq + alpha * alpha * qq
@@ -687,7 +687,7 @@
 def finish(coef_ref, b_ref, q_ref, w_ref, x_hbm, r_hbm, made, out_sem):
     first, second = coef_ref[0:1, 0:1], coef_ref[1:2, 0:1]
     stores = []
-    for part, (start, size) in enumerate(((0, 104), (104, NODES - 104))):
+    for part, (start, size) in enumerate(((0, 40), (40, 56), (96, 56), (152, NODES - 152))):
         rows = pl.ds(start, size)
         b, q, w = b_ref[rows, :], q_ref[rows, :], w_ref[rows, :]
         made[0, rows, :] = first * b - second * q
@@ -761,7 +761,7 @@
             pltpu.VMEM((256, 128), F32),
             pltpu.VMEM((FR, 256), F32),
             pltpu.VMEM((FR, 256), F32),
-            pltpu.VMEM((others, 1, 128), F32),
+            pltpu.VMEM((others, 128), F32),
             pltpu.VMEM((1, 128), F32),
             dma((14,)),
             dma((2, 2)),
@@ -786,7 +786,7 @@
         out_shape=(field, field),
         in_specs=[vmem] * 4,
         out_specs=(hbm, hbm),
-        scratch_shapes=[pltpu.VMEM((2, NODES, ELEMS), F32), dma((2, 2))],
+        scratch_shapes=[pltpu.VMEM((2, NODES, ELEMS), F32), dma((4, 2))],
         compiler_params=pltpu.CompilerParams(vmem_limit_bytes=40 * 1024 * 1024),
     )(coef, right_side, q, w)
 

time: 26.7 us -> 26.6 us (level)
  no operation moved by 1% of the time
where the time goes in v8:
time: 26.6 us; the launch traced here: 26.4 us
  Pallas kernels  25.8 us (97%)
  between operations  0.66 us (2%)
    pallas_call x1, Pallas kernels, body(): pl.pallas_call(functools.partial(kernel, n_gx, n_gy), out_shape=(field, f...  24.7 us
    pallas_call x1, Pallas kernels, body(): pl.pallas_call(finish, out_shape=(field, field), in_specs=[vmem] * 4, out...  1.04 us

profile of v8, /device:TPU:1, one launch (start us, length us, event | category | flops | bytes accessed | tf_op | source)
XLA Modules:
  0.0 26.4 jit_solution(9526422578774302402)
XLA Ops:
  0.6 0.0 copy-start
  0.6 24.7 %shard_map.149 = (f32[216,512]{1,0:T(8,128)S(1)}, f32[216,512]{1,0:T(8,128)S(1)}, f32[8,128]{1,0:T(8,128)S(1)}) custom-call(f32[216,512]{1,0:T(8,128)} %b_ref.1, f32[3,216,216]{2,1,0:T(8,128)} %stiff_hbm.1, f32[3,512]{1,0:T(4,128)} %metric_hbm.1, s32[1,512]{1,0:T(1,128)} %bitcast.9, s32[1,512]{1,0:T(1,128)} %bitcast.10, s32[1,512]{1,0:T(1,128)} %bitcast.11, ...), custom_call_target="tpu_custom_call" | custom-call | tf_op jit(solution)/shard_map/pallas_call | solution.py:737
  25.4 0.0 copy-done
  25.4 1.0 %shard_map.150 = (f32[216,512]{1,0:T(8,128)}, f32[216,512]{1,0:T(8,128)}) custom-call(f32[8,128]{1,0:T(8,128)S(1)} %get-tuple-element.5.coef_ref, f32[216,512]{1,0:T(8,128)S(1)} %copy-done, f32[216,512]{1,0:T(8,128)S(1)} %get-tuple-element.6.q_ref, f32[216,512]{1,0:T(8,128)S(1)} %get-tuple-element.7.w_ref), custom_call_target="tpu_custom_call" | custom-call | tf_op jit(solution)/shard_map/pallas_call | solution.py:784
Async XLA Ops:
  0.6 24.8 %copy-start = (f32[216,512]{1,0:T(8,128)S(1)}, f32[216,512]{1,0:T(8,128)}, u32[]{:S(2)}) copy-start(f32[216,512]{1,0:T(8,128)} %b_ref.1) | copy-start | bytes 1327108
